TPU v7x, 32 devices: a whole 2x2x4 slice. The times are simulated.
32 devices in a mesh: grp: 2 (over y), ft: 4 (over z), bl: 4 (over x, core).
Axes of the slice: x: 2, y: 2, z: 4, core: 2. Of those that a mesh axis runs over, the one named last changes fastest.
Arguments:
- voltages: bfloat16 [2, 16384, 1024], P(None, ('grp', 'ft'), 'bl'), parts along dimension 1, may hold values from -11 to 11
- coefs: float32 [8, 2048], replicated, may hold values from -2 to 2
- block_ids: int32 [4], replicated, may hold values from 0 to 3, each once
- tile_owner: int32 [20], P('grp'), parts along dimension 0, may hold values from 0 to 3, as said below
Outputs:
- vis: float32 [2, 64, 20, 256, 256], P(None, ('grp', 'ft'), 'bl'), parts along dimension 1
There are 2 independent parts, one for each index of `grp`. A program takes and returns all parts, laid end to end along the dimension named above; an argument that names none is the same for every part. Nothing has to cross between parts.
Inputs may be any that keep to these rules, and one draw needn't show every extreme that they name: tile_owner[t] is the index along bl of the device that owns tile t; one owner holds exactly 5 tiles, the others share the remaining tiles as evenly as counts allow.
All inputs are finite; a program needn't handle non-finite values.
Results may differ from a plain program's by a relative error of at most 0.00099.
Values may be sent and summed in bfloat16 or wider, within the bound.
No kernel may reach another device: no remote copies, remote signals or barrier semaphores. Data moves between devices by JAX's collectives and lax.ppermute only.
A program may use at most 128 MiB of HBM per device.

v0:
```python
import functools
import math

import jax
import jax.numpy as jnp
import ml_dtypes
import numpy as np
from jax import lax
from jax.experimental import pallas as pl
from jax.experimental.pallas import tpu as pltpu
from jax.sharding import PartitionSpec as P

AVG = 64
MXU = 256
LANES = 128
ROWS16 = 16
VMEM_BYTES = 48 * 1024 * 1024


def split_bf16(table):
    high = table.astype(ml_dtypes.bfloat16)
    low = (table - high.astype(np.float64)).astype(ml_dtypes.bfloat16)
    return high, low


def matrix_tables(inner_len):
    steps = np.arange(inner_len)
    angles = 2.0 * np.pi * (np.outer(steps, steps) % inner_len) / inner_len
    cos_part, sin_part = np.cos(angles), np.sin(angles)
    return split_bf16(np.block([[cos_part, -sin_part], [sin_part, cos_part]]))


def twiddle_tables(radix, inner_len):
    chan_count = radix * inner_len
    angles = 2.0 * np.pi * np.outer(np.arange(radix), np.arange(inner_len)) / chan_count
    scale = 1.0 / math.sqrt(chan_count)
    return np.stack([np.cos(angles) * scale, np.sin(angles) * scale]).astype(np.float32)


def rotate(real, imag, step, count):
    step = step % count
    if step == 0:
        return real, imag
    if 4 * step == count:
        return imag, -real
    if 2 * step == count:
        return -real, -imag
    if 4 * step == 3 * count:
        return -imag, real
    cos_step = math.cos(2.0 * math.pi * step / count)
    sin_step = math.sin(2.0 * math.pi * step / count)
    if 8 * step == count:
        return cos_step * (real + imag), cos_step * (imag - real)
    return cos_step * real + sin_step * imag, cos_step * imag - sin_step * real


def butterflies(parts):
    count = len(parts)
    if count == 1:
        return parts
    half = count // 2
    sums, diffs = [], []
    for k in range(half):
        (ar, ai), (br, bi) = parts[k], parts[k + half]
        sums.append((ar + br, ai + bi))
        diffs.append(rotate(ar - br, ai - bi, k, count))
    even, odd = butterflies(sums), butterflies(diffs)
    out = []
    for k in range(half):
        out += [even[k], odd[k]]
    return out


def pack_kernel(radix, place_ref, v_ref, *rest):
    o_refs, (wide, turned) = rest[:-2], rest[-2:]
    dests, rows, samples = turned.shape
    inner = samples // radix
    wide[...] = v_ref[0].astype(jnp.float32)
    for phase in range(radix):
        part = wide[pl.ds(phase, inner, stride=radix), :].T.astype(jnp.bfloat16)
        for dest in range(dests):
            turned[dest, :, phase * inner : (phase + 1) * inner] = part[
                dest * rows : (dest + 1) * rows
            ]
    for shift in range(dests):
        o_refs[shift][0] = turned[place_ref[shift]]


def pack(voltages, place, chunk, dests, radix):
    _, samples, _ = voltages.shape
    rows = LANES // dests
    return pl.pallas_call(
        functools.partial(pack_kernel, radix),
        grid_spec=pltpu.PrefetchScalarGridSpec(
            num_scalar_prefetch=1,
            grid=(2,),
            in_specs=[pl.BlockSpec((1, samples, LANES), lambda p, t: (p, 0, chunk))],
            out_specs=[pl.BlockSpec((1, rows, samples), lambda p, t: (p, 0, 0))] * dests,
            scratch_shapes=[
                pltpu.VMEM((samples, LANES), jnp.float32),
                pltpu.VMEM((dests, rows, samples), jnp.bfloat16),
            ],
        ),
        out_shape=[jax.ShapeDtypeStruct((2, rows, samples), jnp.bfloat16)] * dests,
        compiler_params=pltpu.CompilerParams(vmem_limit_bytes=VMEM_BYTES),
        name="pack_inputs",
    )(place, voltages)


def transform_kernel(radix, dests, place_ref, *rest):
    v_refs = rest[:dests]
    c_ref, gh_ref, gl_ref, tw_ref = rest[dests : dests + 4]
    out_refs, (held, split, prod) = rest[dests + 4 : -3], rest[-3:]
    spectra, _, rows, samples = held.shape
    taps = c_ref.shape[0]
    inner = samples // radix
    group = spectra * rows
    for shift in range(dests):
        held[place_ref[dests + shift]] = v_refs[shift][...]

    @pl.loop(0, radix)
    def _(phase):
        lane0 = pl.multiple_of(phase * inner, inner)
        row0 = pl.multiple_of(phase * group, group)
        for part in range(2):
            for sub in range(0, rows, ROWS16):
                blocks = [
                    held[b, part, pl.ds(sub, ROWS16), pl.ds(lane0, inner)].astype(jnp.float32)
                    for b in range(spectra)
                ]
                for s in range(spectra):
                    total = None
                    for b in range(max(0, s - taps + 1), s + 1):
                        term = c_ref[taps - 1 - s + b, pl.ds(phase, 1), :] * blocks[b]
                        total = term if total is None else total + term
                    high = total.astype(jnp.bfloat16)
                    low = (total - high.astype(jnp.float32)).astype(jnp.bfloat16)
                    at = pl.ds(pl.multiple_of(row0 + s * rows + sub, ROWS16), ROWS16)
                    split[at, part * inner : (part + 1) * inner] = high
                    split[at, (2 + part) * inner : (3 + part) * inner] = low

    high = split[:, : 2 * inner]
    prod[...] = (
        jnp.dot(high, gh_ref[...], preferred_element_type=jnp.float32)
        + jnp.dot(high, gl_ref[...], preferred_element_type=jnp.float32)
        + jnp.dot(split[:, 2 * inner :], gh_ref[...], preferred_element_type=jnp.float32)
    )

    halves = len(out_refs)

    @pl.loop(0, spectra)
    def _(s):
        for sub in range(0, rows, ROWS16):
            for lane in range(0, inner, LANES):
                parts = []
                for phase in range(radix):
                    at = pl.ds(pl.multiple_of(phase * group + s * rows + sub, ROWS16), ROWS16)
                    yr = prod[at, lane : lane + LANES]
                    yi = prod[at, inner + lane : inner + lane + LANES]
                    cos_here = tw_ref[0, phase : phase + 1, lane : lane + LANES]
                    sin_here = tw_ref[1, phase : phase + 1, lane : lane + LANES]
                    if phase == 0:
                        parts.append((yr * cos_here, yi * cos_here))
                    else:
                        parts.append(
                            (yr * cos_here + yi * sin_here, yi * cos_here - yr * sin_here)
                        )
                for step, pair in enumerate(butterflies(parts)):
                    for part in range(2):
                        out_refs[step % halves][
                            step // halves, part, s, sub : sub + ROWS16, lane : lane + LANES
                        ] = pair[part].astype(jnp.bfloat16)


def transform_chunk(blocks, place, coef_table, radix):
    dests = len(blocks)
    _, rows, samples = blocks[0].shape
    spectra = dests
    inner = samples // radix
    halves = radix // dests
    g_high, g_low = matrix_tables(inner)
    vmem = pl.BlockSpec(memory_space=pltpu.VMEM)
    total = radix * spectra * rows
    return pl.pallas_call(
        functools.partial(transform_kernel, radix, dests),
        grid_spec=pltpu.PrefetchScalarGridSpec(
            num_scalar_prefetch=1,
            grid=(),
            in_specs=[vmem] * (dests + 4),
            out_specs=[vmem] * halves,
            scratch_shapes=[
                pltpu.VMEM((spectra, 2, rows, samples), jnp.bfloat16),
                pltpu.VMEM((total, 4 * inner), jnp.bfloat16),
                pltpu.VMEM((total, 2 * inner), jnp.float32),
            ],
        ),
        out_shape=[jax.ShapeDtypeStruct((dests, 2, spectra, rows, inner), jnp.bfloat16)]
        * halves,
        cost_estimate=pl.CostEstimate(
            flops=3 * 2 * total * 4 * inner * inner, bytes_accessed=6 << 20, transcendentals=0
        ),
        compiler_params=pltpu.CompilerParams(vmem_limit_bytes=VMEM_BYTES),
        name="filter_transform",
    )(
        place,
        *blocks,
        coef_table,
        jnp.asarray(g_high),
        jnp.asarray(g_low),
        twiddle_tables(radix, inner),
    )


def correlate_kernel(chunks, blocks, scale, table_ref, *rest):
    g_refs, o_ref, left = rest[: chunks * blocks], rest[-2], rest[-1]
    senders, _, spectra, rows, inner = g_refs[0].shape
    slots = o_ref.shape[2]
    coarse = inner // AVG
    side = chunks * senders * rows
    step = pl.program_id(0)

    @pl.when(step == 0)
    def _():
        for chunk in range(chunks):
            for block in range(blocks):
                source = g_refs[chunk * blocks + block]

                @pl.loop(0, senders)
                def _(shift, chunk=chunk, block=block, source=source):
                    sender = shift
                    row = pl.multiple_of((chunk * senders + sender) * rows, rows)
                    for part in range(2):
                        pieces = [source[shift, part, s] for s in range(spectra)]
                        for c in range(coarse):
                            line = jnp.concatenate(
                                [piece[:, c * AVG : (c + 1) * AVG] for piece in pieces], axis=1
                            )
                            width = line.shape[1]
                            left[
                                c, block, pl.ds(row, rows), part * width : (part + 1) * width
                            ] = line
                            left[
                                c,
                                block,
                                pl.ds(pl.multiple_of(side + row, rows), rows),
                                (1 - part) * width : (2 - part) * width,
                            ] = -line if part == 0 else line

    count = table_ref[2 * slots]
    for slot in range(slots):

        @pl.when(slot < count)
        def _(slot=slot):
            rows_of = left[step, table_ref[slot]]
            cols_of = left[step, table_ref[slots + slot], pl.ds(0, side), :]
            tile = (
                lax.dot_general(
                    rows_of,
                    cols_of,
                    (((1,), (1,)), ((), ())),
                    preferred_element_type=jnp.float32,
                )
                * scale
            )
            o_ref[0, 0, slot] = tile[:side]
            o_ref[1, 0, slot] = tile[side:]

        @pl.when(slot >= count)
        def _(slot=slot):
            o_ref[:, 0, slot] = jnp.zeros((2, side, side), jnp.float32)


def correlate(table, gathered, part_index, part_count, slots, vis):
    chunks, blocks = len(gathered), len(gathered[0])
    senders, _, spectra, rows, inner = gathered[0][0].shape
    coarse = inner // AVG
    side = chunks * senders * rows
    scale = 1.0 / (AVG * spectra)
    parts = [block for chunk in gathered for block in chunk]
    in_specs = [
        pl.BlockSpec(part.shape, lambda c, t: (0,) * 5, pipeline_mode=pl.Buffered(1))
        for part in parts
    ]
    args = [table, *parts]
    aliases = {}
    if vis is not None:
        in_specs.append(pl.BlockSpec(memory_space=pl.ANY))
        args.append(vis)
        aliases = {len(args) - 1: 0}
    return pl.pallas_call(
        functools.partial(correlate_kernel, chunks, blocks, scale),
        grid_spec=pltpu.PrefetchScalarGridSpec(
            num_scalar_prefetch=1,
            grid=(coarse,),
            in_specs=in_specs,
            out_specs=pl.BlockSpec(
                (2, 1, slots, side, side), lambda c, t: (0, part_index * coarse + c, 0, 0, 0)
            ),
            scratch_shapes=[
                pltpu.VMEM((coarse, blocks, 2 * side, 2 * spectra * AVG), jnp.bfloat16)
            ],
        ),
        out_shape=jax.ShapeDtypeStruct(
            (2, part_count * coarse, slots, side, side), jnp.float32
        ),
        input_output_aliases=aliases,
        cost_estimate=pl.CostEstimate(
            flops=coarse * slots * 2 * 4 * side * side * spectra * AVG,
            bytes_accessed=16 << 20,
            transcendentals=0,
        ),
        compiler_params=pltpu.CompilerParams(vmem_limit_bytes=VMEM_BYTES),
        name="correlate_tiles",
    )(*args)


def places(count):
    steps = np.arange(count, dtype=np.int32)
    index = lax.axis_index("ft").astype(jnp.int32)
    return jnp.concatenate([(index + steps) % count, (index + count - steps) % count])


def spread(pieces):
    count = len(pieces)
    return [pieces[0]] + [
        lax.ppermute(pieces[d], "ft", [(i, (i + d) % count) for i in range(count)])
        for d in range(1, count)
    ]


def gather_blocks(own):
    count = lax.axis_size("bl")
    held = {0: own}
    bit = count // 2
    while bit:
        for r in list(held):
            held[r ^ bit] = lax.ppermute(held[r], "bl", [(i, i ^ bit) for i in range(count)])
        bit //= 2
    return [held[r] for r in range(count)]


def tile_tables(block_ids, tile_owner, place):
    block_count = lax.axis_size("bl")
    tile_count = block_count * (block_count + 1) // 2
    slot_cap = 2 * tile_count // block_count
    pairs = [(i, j) for i in range(block_count) for j in range(i, block_count)]
    row_table = np.array([i for i, _ in pairs], np.int32)
    col_table = np.array([j for _, j in pairs], np.int32)
    mine = (tile_owner == lax.axis_index("bl")).astype(jnp.int32)
    earlier = np.tril(np.ones((tile_count, tile_count), np.int32), -1)
    rank = jnp.sum(earlier * mine[None, :], axis=1)
    labels = np.arange(block_count, dtype=np.int32)
    shard_of = jnp.sum(jnp.where(block_ids[None, :] == labels[:, None], labels[None, :], 0), axis=1)
    row_shard = jnp.sum(
        jnp.where(row_table[:, None] == labels[None, :], shard_of[None, :], 0), axis=1
    )
    col_shard = jnp.sum(
        jnp.where(col_table[:, None] == labels[None, :], shard_of[None, :], 0), axis=1
    )
    here = (mine[None, :] == 1) & (rank[None, :] == np.arange(slot_cap, dtype=np.int32)[:, None])
    rows = jnp.sum(jnp.where(here, row_shard[None, :], 0), axis=1)
    cols = jnp.sum(jnp.where(here, col_shard[None, :], 0), axis=1)
    index = lax.axis_index("bl")
    table = jnp.concatenate(
        [rows ^ index, cols ^ index, jnp.sum(mine, keepdims=True), place]
    ).astype(jnp.int32)
    return table, slot_cap


def takes_kernels(mesh, voltages, coefs):
    dests = mesh.shape["ft"]
    blocks = mesh.shape["bl"]
    inputs = voltages.shape[2] // mesh.shape["bl"]
    per_dev = voltages.shape[1] // (mesh.shape["grp"] * dests)
    chan_count = coefs.shape[1]
    radix = chan_count // MXU
    return (
        per_dev == chan_count
        and chan_count % MXU == 0
        and radix & (radix - 1) == 0
        and radix % dests == 0
        and radix <= 8
        and blocks & (blocks - 1) == 0
        and inputs % LANES == 0
        and LANES % dests == 0
        and (LANES // dests) % ROWS16 == 0
        and (dests * AVG) % LANES == 0
    )


def per_device_kernels(voltages, coefs, block_ids, tile_owner):
    dests = lax.axis_size("ft")
    taps, chan_count = coefs.shape
    radix = chan_count // MXU
    chunk_count = voltages.shape[2] // LANES
    halves = radix // dests
    coef_table = coefs.reshape(taps, MXU, radix).transpose(0, 2, 1)
    place = places(dests)
    table, slot_cap = tile_tables(block_ids, tile_owner, place)
    arrived = [
        spread(pack(voltages, place, chunk, dests, radix)) for chunk in range(chunk_count)
    ]
    gathered = [[] for _ in range(halves)]
    for chunk in range(chunk_count):
        for half, parts in enumerate(transform_chunk(arrived[chunk], place, coef_table, radix)):
            turned = lax.all_to_all(parts, "ft", split_axis=0, concat_axis=0, tiled=True)
            gathered[half].append(gather_blocks(turned))
    vis = None
    for half in range(halves):
        vis = correlate(table, gathered[half], half, halves, slot_cap, vis)
    return vis


def tile_product(row_part, col_part, norm_scale):
    products = jnp.einsum(
        "pscax,qscay->cpqxy", row_part, col_part, preferred_element_type=jnp.float32
    )
    real_part = products[:, 0, 0] + products[:, 1, 1]
    imag_part = products[:, 1, 0] - products[:, 0, 1]
    return jnp.stack([real_part, imag_part]) * norm_scale


def dft_tables(order_len):
    steps_one = jnp.arange(order_len, dtype=jnp.int32)
    phase_grid = steps_one[:, None] * steps_one[None, :] % order_len
    angles = phase_grid.astype(jnp.float32) * (2.0 * math.pi / order_len)
    return (jnp.cos(angles), jnp.sin(angles))


def transform(filtered):
    per_dev = filtered.shape[1]
    chan_count = filtered.shape[2]
    rows_here = filtered.shape[3]
    outer_len = math.isqrt(chan_count)
    while chan_count % outer_len != 0:
        outer_len = outer_len - 1
    inner_len = chan_count // outer_len
    highest = lax.Precision.HIGHEST
    reshaped = filtered.reshape(2, per_dev, outer_len, inner_len, rows_here)
    real_in = reshaped[0]
    imag_in = reshaped[1]
    cos_outer, sin_outer = dft_tables(outer_len)
    section_re = jnp.einsum("snkb,nm->smkb", real_in, cos_outer, precision=highest) + jnp.einsum(
        "snkb,nm->smkb", imag_in, sin_outer, precision=highest
    )
    section_im = jnp.einsum("snkb,nm->smkb", imag_in, cos_outer, precision=highest) - jnp.einsum(
        "snkb,nm->smkb", real_in, sin_outer, precision=highest
    )
    twiddle_grid = (
        jnp.arange(outer_len, dtype=jnp.int32)[:, None]
        * jnp.arange(inner_len, dtype=jnp.int32)[None, :]
        % chan_count
    )
    twiddle_angles = twiddle_grid.astype(jnp.float32) * (2.0 * math.pi / chan_count)
    cos_twiddle = jnp.cos(twiddle_angles)[None, :, :, None]
    sin_twiddle = jnp.sin(twiddle_angles)[None, :, :, None]
    rot_re = section_re * cos_twiddle + section_im * sin_twiddle
    rot_im = section_im * cos_twiddle - section_re * sin_twiddle
    cos_inner, sin_inner = dft_tables(inner_len)
    final_re = jnp.einsum("smkb,kq->sqmb", rot_re, cos_inner, precision=highest) + jnp.einsum(
        "smkb,kq->sqmb", rot_im, sin_inner, precision=highest
    )
    final_im = jnp.einsum("smkb,kq->sqmb", rot_im, cos_inner, precision=highest) - jnp.einsum(
        "smkb,kq->sqmb", rot_re, sin_inner, precision=highest
    )
    stacked = jnp.stack([final_re, final_im]).reshape(2, per_dev, chan_count, rows_here)
    return (stacked * (1.0 / math.sqrt(chan_count))).astype(jnp.bfloat16)


def apply_taps(window, coef_part, taps_count, out_len):
    filtered = jnp.zeros((2, out_len, window.shape[2], window.shape[3]), jnp.float32)
    for tap_index in range(taps_count):
        filtered = filtered + coef_part[tap_index][None, None, :, None] * window[
            :, tap_index : tap_index + out_len
        ].astype(jnp.float32)
    return filtered


def per_device(voltages, coefs, block_ids, tile_owner):
    taps_count = coefs.shape[0]
    chan_count = coefs.shape[1]
    rows_here = voltages.shape[2]
    per_dev = voltages.shape[1] // chan_count
    volt_blocks = voltages.reshape(2, per_dev, chan_count, rows_here)
    phase_block = lax.all_to_all(volt_blocks, "ft", split_axis=2, concat_axis=1, tiled=True)
    spectra_count = phase_block.shape[1]
    phase_here = phase_block.shape[2]
    coef_part = lax.dynamic_slice_in_dim(coefs, lax.axis_index("ft") * phase_here, phase_here, 1)
    zero_front = jnp.zeros((2, taps_count - 1, phase_here, rows_here), phase_block.dtype)
    long_window = jnp.concatenate([zero_front, phase_block], axis=1)
    phase_filtered = apply_taps(long_window, coef_part, taps_count, spectra_count)
    filtered = lax.all_to_all(phase_filtered, "ft", split_axis=1, concat_axis=2, tiled=True)
    spectra = transform(filtered)
    turned = lax.all_to_all(spectra, "ft", split_axis=2, concat_axis=1, tiled=True)
    spectra_all = turned.shape[1]
    chan_here = turned.shape[2]
    coarse_here = chan_here // AVG
    coarse_view = turned.reshape(2, spectra_all, coarse_here, AVG, rows_here)
    norm_scale = 1.0 / (AVG * spectra_all)
    block_count = lax.axis_size("bl")
    my_index = lax.axis_index("bl")
    tile_count = block_count * (block_count + 1) // 2
    slot_cap = 2 * tile_count // block_count
    row_table = jnp.asarray(
        np.array(
            [
                first_id
                for first_id in range(block_count)
                for second_id in range(first_id, block_count)
            ],
            dtype=np.int32,
        )
    )
    col_table = jnp.asarray(
        np.array(
            [
                second_id
                for first_id in range(block_count)
                for second_id in range(first_id, block_count)
            ],
            dtype=np.int32,
        )
    )
    tile_pos = jnp.arange(tile_count, dtype=jnp.int32)
    same_owner = tile_owner[None, :] == tile_owner[:, None]
    before_mask = tile_pos[None, :] < tile_pos[:, None]
    slot_rank = jnp.sum((same_owner & before_mask).astype(jnp.int32), axis=1)
    labels = jnp.arange(block_count, dtype=jnp.int32)
    shard_of = jnp.sum(jnp.where(block_ids[None, :] == labels[:, None], labels[None, :], 0), axis=1)
    gathered = lax.all_gather(coarse_view[None], "bl", axis=0, tiled=True)
    mine_mask = tile_owner == my_index
    own_count = jnp.sum(mine_mask.astype(jnp.int32))
    slot_steps = jnp.arange(slot_cap, dtype=jnp.int32)
    slot_tile = jnp.sum(
        jnp.where(
            mine_mask[None, :] & (slot_rank[None, :] == slot_steps[:, None]), tile_pos[None, :], 0
        ),
        axis=1,
    )

    def one_tile(slot_pos, result_tiles):
        tile_id = slot_tile[slot_pos]
        row_block = gathered[shard_of[row_table[tile_id]]]
        col_block = gathered[shard_of[col_table[tile_id]]]
        tile = tile_product(row_block, col_block, norm_scale)
        return lax.dynamic_update_slice(result_tiles, tile[:, :, None], (0, 0, slot_pos, 0, 0))

    empty_tiles = jnp.zeros((2, coarse_here, slot_cap, rows_here, rows_here), jnp.float32)
    return lax.fori_loop(0, own_count, one_tile, empty_tiles)


def solution(mesh):
    def correlator(voltages, coefs, block_ids, tile_owner):
        fits = takes_kernels(mesh, voltages, coefs)
        return jax.shard_map(
            per_device_kernels if fits else per_device,
            mesh=mesh,
            in_specs=(P(None, ("grp", "ft"), "bl"), P(), P(), P("grp")),
            out_specs=P(None, ("grp", "ft"), "bl", None, None),
            check_vma=False,
        )(voltages, coefs, block_ids, tile_owner)

    return correlator
```

profile of v0, /device:TPU:15, one launch (start us, length us, event | category | flops | bytes accessed | tf_op | source)
XLA Modules:
  0.0 196.8 jit_solution(14744182633033425894)
XLA Ops:
  0.1 0.1 pad_add_fusion.place_ref
  0.1 1.6 copy-done
  1.7 1.4 pack_inputs.3
  3.1 1.3 collective-permute-start.6
  4.5 1.1 collective-permute-start.7
  5.6 1.4 collective-permute-start.8
  7.0 1.4 reshape.11
  8.4 0.3 copy.20
  8.7 1.7 collective-permute-done.6.rest_1_
  10.4 15.9 %collective-permute-done.7.rest_2_ = bf16[2,32,2048]{2,1,0:T(8,128)(2,1)S(1)} collective-permute-done((bf16[2,32,2048]{2,1,0:T(8,128)(2,1)S(1)}, bf16[2,32,2048]{2,1,0:T(8,128)(2,1)S(1)}, u32[]{:S(2)}, u32[]{:S(2)}) %collective-permute-start.7) | collective-permute-done | bytes 262176 | tf_op jit(solution)/shard_map/ppermute | solution.py:326
  26.3 2.8 %collective-permute-done.8.rest_3_ = bf16[2,32,2048]{2,1,0:T(8,128)(2,1)S(1)} collective-permute-done((bf16[2,32,2048]{2,1,0:T(8,128)(2,1)S(1)}, bf16[2,32,2048]{2,1,0:T(8,128)(2,1)S(1)}, u32[]{:S(2)}, u32[]{:S(2)}) %collective-permute-start.8) | collective-permute-done | bytes 262176 | tf_op jit(solution)/shard_map/ppermute | solution.py:326
  29.2 1.0 copy-done.4
  30.2 1.0 copy-done.6
  31.2 0.7 copy-done.8
  32.0 4.4 %filter_transform.3 = (bf16[4,2,4,32,256]{4,3,2,1,0:T(8,128)(2,1)}, bf16[4,2,4,32,256]{4,3,2,1,0:T(8,128)(2,1)S(1)}) custom-call(s32[8]{0:T(128)S(1)} %pad_add_fusion.place_ref, bf16[2,32,2048]{2,1,0:T(8,128)(2,1)S(1)} %get-tuple-element.22.rest_0_, bf16[2,32,2048]{2,1,0:T(8,128)(2,1)S(1)} %collective-permute-done.6.rest_1_, ...), custom_call_target="tpu_custom_call" | custom-call | flops 1610612736 | bytes 6291456 | tf_op jit(solution)/shard_map/filter_transform/pallas_call | solution.py:184
  36.3 13.8 %all_to_all.20.rest_4_ = bf16[4,2,4,32,256]{4,3,2,1,0:T(8,128)(2,1)S(1)} all-to-all(bf16[4,2,4,32,256]{4,3,2,1,0:T(8,128)(2,1)S(1)} %get-tuple-element.26), channel_id=1, replica_groups=mesh['grp'=2,'ft'=4,'bl'=4] {'ft'}, dimensions={0} | all-to-all | bytes 1048576 | tf_op jit(solution)/shard_map/all_to_all | solution.py:406
  50.2 5.7 %all-to-all-start.3 = ((bf16[4,2,4,32,256]{4,3,2,1,0:T(8,128)(2,1)}), bf16[4,2,4,32,256]{4,3,2,1,0:T(8,128)(2,1)S(1)}, u32[]{:S(2)}, u32[]{:S(2)}) async-start(bf16[4,2,4,32,256]{4,3,2,1,0:T(8,128)(2,1)} %get-tuple-element.28), calls=%async_computation.3 | async-start | bytes 1048576 | tf_op jit(solution)/shard_map/all_to_all | solution.py:406
  55.9 1.6 copy-done.1
  57.5 1.4 pack_inputs.2
  58.9 1.2 collective-permute-start
  60.1 1.0 collective-permute-start.1
  61.1 1.4 collective-permute-start.2
  62.5 20.8 %collective-permute-done.rest_1_ = bf16[2,32,2048]{2,1,0:T(8,128)(2,1)S(1)} collective-permute-done((bf16[2,32,2048]{2,1,0:T(8,128)(2,1)S(1)}, bf16[2,32,2048]{2,1,0:T(8,128)(2,1)S(1)}, u32[]{:S(2)}, u32[]{:S(2)}) %collective-permute-start) | collective-permute-done | bytes 262176 | tf_op jit(solution)/shard_map/ppermute | solution.py:326
  83.2 5.6 %collective-permute-done.1.rest_2_ = bf16[2,32,2048]{2,1,0:T(8,128)(2,1)S(1)} collective-permute-done((bf16[2,32,2048]{2,1,0:T(8,128)(2,1)S(1)}, bf16[2,32,2048]{2,1,0:T(8,128)(2,1)S(1)}, u32[]{:S(2)}, u32[]{:S(2)}) %collective-permute-start.1) | collective-permute-done | bytes 262176 | tf_op jit(solution)/shard_map/ppermute | solution.py:326
  88.8 2.3 %collective-permute-done.2.rest_3_ = bf16[2,32,2048]{2,1,0:T(8,128)(2,1)S(1)} collective-permute-done((bf16[2,32,2048]{2,1,0:T(8,128)(2,1)S(1)}, bf16[2,32,2048]{2,1,0:T(8,128)(2,1)S(1)}, u32[]{:S(2)}, u32[]{:S(2)}) %collective-permute-start.2) | collective-permute-done | bytes 262176 | tf_op jit(solution)/shard_map/ppermute | solution.py:326
  91.1 1.0 copy-done.5
  92.2 1.0 copy-done.7
  93.2 0.7 copy-done.9
  93.9 4.4 %filter_transform.2 = (bf16[4,2,4,32,256]{4,3,2,1,0:T(8,128)(2,1)S(1)}, bf16[4,2,4,32,256]{4,3,2,1,0:T(8,128)(2,1)}) custom-call(s32[8]{0:T(128)S(1)} %pad_add_fusion.place_ref, bf16[2,32,2048]{2,1,0:T(8,128)(2,1)S(1)} %get-tuple-element.17.rest_0_, bf16[2,32,2048]{2,1,0:T(8,128)(2,1)S(1)} %collective-permute-done.rest_1_, ...), custom_call_target="tpu_custom_call" | custom-call | flops 1610612736 | bytes 6291456 | tf_op jit(solution)/shard_map/filter_transform/pallas_call | solution.py:184
  98.3 0.0 all-to-all-done.3.rest_4_
  98.3 13.9 %all_to_all.21.rest_0_ = bf16[4,2,4,32,256]{4,3,2,1,0:T(8,128)(2,1)S(1)} all-to-all(bf16[4,2,4,32,256]{4,3,2,1,0:T(8,128)(2,1)S(1)} %get-tuple-element.27), channel_id=1, replica_groups=mesh['grp'=2,'ft'=4,'bl'=4] {'ft'}, dimensions={0} | all-to-all | bytes 1048576 | tf_op jit(solution)/shard_map/all_to_all | solution.py:406
  112.3 6.0 %all-to-all-start = ((bf16[4,2,4,32,256]{4,3,2,1,0:T(8,128)(2,1)}), bf16[4,2,4,32,256]{4,3,2,1,0:T(8,128)(2,1)S(1)}, u32[]{:S(2)}, u32[]{:S(2)}) async-start(bf16[4,2,4,32,256]{4,3,2,1,0:T(8,128)(2,1)} %get-tuple-element.21), calls=%async_computation | async-start | bytes 1048576 | tf_op jit(solution)/shard_map/all_to_all | solution.py:406
  118.3 0.3 collective-permute-start.16
  118.5 2.6 %collective-permute-start.15 = (bf16[4,2,4,32,256]{4,3,2,1,0:T(8,128)(2,1)S(1)}, bf16[4,2,4,32,256]{4,3,2,1,0:T(8,128)(2,1)}, u32[]{:S(2)}, u32[]{:S(2)}) collective-permute-start(bf16[4,2,4,32,256]{4,3,2,1,0:T(8,128)(2,1)S(1)} %all-to-all-done.3.rest_4_), channel_id=1, source_target_pairs={{0,1},{1,0},{2,3},{3,2},{4,5},{5,4},{6,7},{7,6},{8,9},{9,8},{10,11... | collective-permute-start | bytes 1572872 | tf_op jit(solution)/shard_map/ppermute | solution.py:337
  121.1 1.2 collective-permute-start.13
  122.3 0.7 fusion.4
  123.0 0.3 collective-permute-start.12
  123.3 0.3 collective-permute-start.10
  123.5 5.3 %all-to-all-done.rest_0_ = bf16[4,2,4,32,256]{4,3,2,1,0:T(8,128)(2,1)S(1)} async-done(((bf16[4,2,4,32,256]{4,3,2,1,0:T(8,128)(2,1)}), bf16[4,2,4,32,256]{4,3,2,1,0:T(8,128)(2,1)S(1)}, u32[]{:S(2)}, u32[]{:S(2)}) %all-to-all-start) | async-done | bytes 524320 | tf_op jit(solution)/shard_map/all_to_all | solution.py:406
  128.9 0.6 collective-permute-done.16.rest_6_
  129.5 0.3 collective-permute-start.4
  129.8 0.0 collective-permute-done.15.rest_5_
  129.8 6.3 %collective-permute-start.17 = (bf16[4,2,4,32,256]{4,3,2,1,0:T(8,128)(2,1)}, bf16[4,2,4,32,256]{4,3,2,1,0:T(8,128)(2,1)S(1)}, u32[]{:S(2)}, u32[]{:S(2)}) collective-permute-start(bf16[4,2,4,32,256]{4,3,2,1,0:T(8,128)(2,1)} %collective-permute-done.16.rest_6_), channel_id=1, source_target_pairs={{0,1},{1,0},{2,3},{3,2},{4,5},{5,4},{6,7},{7,6},{8,9},{9,8},{10,11... | collective-permute-start | bytes 1572872 | tf_op jit(solution)/shard_map/ppermute | solution.py:337
  136.1 0.1 fusion.1
  136.2 0.1 multiply_reduce_fusion
  136.3 0.1 select_reduce_fusion.2
  136.4 4.4 %collective-permute-done.13.rest_2_ = bf16[4,2,4,32,256]{4,3,2,1,0:T(8,128)(2,1)} collective-permute-done((bf16[4,2,4,32,256]{4,3,2,1,0:T(8,128)(2,1)S(1)}, bf16[4,2,4,32,256]{4,3,2,1,0:T(8,128)(2,1)}, u32[]{:S(2)}, u32[]{:S(2)}) %collective-permute-start.13) | collective-permute-done | bytes 524320 | tf_op jit(solution)/shard_map/ppermute | solution.py:337
  140.8 6.0 %collective-permute-start.14 = (bf16[4,2,4,32,256]{4,3,2,1,0:T(8,128)(2,1)}, bf16[4,2,4,32,256]{4,3,2,1,0:T(8,128)(2,1)}, u32[]{:S(2)}, u32[]{:S(2)}) collective-permute-start(bf16[4,2,4,32,256]{4,3,2,1,0:T(8,128)(2,1)} %collective-permute-done.13.rest_2_), channel_id=1, source_target_pairs={{0,1},{1,0},{2,3},{3,2},{4,5},{5,4},{6,7},{7,6},{8,9},{9,8},{10,11... | collective-permute-start | bytes 1572872 | tf_op jit(solution)/shard_map/ppermute | solution.py:337
  146.8 5.1 %collective-permute-done.10.rest_6_ = bf16[4,2,4,32,256]{4,3,2,1,0:T(8,128)(2,1)S(1)} collective-permute-done((bf16[4,2,4,32,256]{4,3,2,1,0:T(8,128)(2,1)S(1)}, bf16[4,2,4,32,256]{4,3,2,1,0:T(8,128)(2,1)S(1)}, u32[]{:S(2)}, u32[]{:S(2)}) %collective-permute-start.10) | collective-permute-done | bytes 524320 | tf_op jit(solution)/shard_map/ppermute | solution.py:337
  151.9 6.0 %collective-permute-start.9 = (bf16[4,2,4,32,256]{4,3,2,1,0:T(8,128)(2,1)S(1)}, bf16[4,2,4,32,256]{4,3,2,1,0:T(8,128)(2,1)}, u32[]{:S(2)}, u32[]{:S(2)}) collective-permute-start(bf16[4,2,4,32,256]{4,3,2,1,0:T(8,128)(2,1)S(1)} %all_to_all.20.rest_4_), channel_id=1, source_target_pairs={{0,1},{1,0},{2,3},{3,2},{4,5},{5,4},{6,7},{7,6},{8,9},{9,8},{10,11... | collective-permute-start | bytes 1572872 | tf_op jit(solution)/shard_map/ppermute | solution.py:337
  157.9 0.0 collective-permute-start.3
  157.9 5.2 %collective-permute-done.4.rest_2_ = bf16[4,2,4,32,256]{4,3,2,1,0:T(8,128)(2,1)S(1)} collective-permute-done((bf16[4,2,4,32,256]{4,3,2,1,0:T(8,128)(2,1)S(1)}, bf16[4,2,4,32,256]{4,3,2,1,0:T(8,128)(2,1)S(1)}, u32[]{:S(2)}, u32[]{:S(2)}) %collective-permute-start.4) | collective-permute-done | bytes 524320 | tf_op jit(solution)/shard_map/ppermute | solution.py:337
  163.1 3.2 %collective-permute-start.11 = (bf16[4,2,4,32,256]{4,3,2,1,0:T(8,128)(2,1)S(1)}, bf16[4,2,4,32,256]{4,3,2,1,0:T(8,128)(2,1)}, u32[]{:S(2)}, u32[]{:S(2)}) collective-permute-start(bf16[4,2,4,32,256]{4,3,2,1,0:T(8,128)(2,1)S(1)} %collective-permute-done.10.rest_6_), channel_id=1, source_target_pairs={{0,1},{1,0},{2,3},{3,2},{4,5},{5,4},{6,7},{7,6},{8,9},{9,8},{10,11... | collective-permute-start | bytes 1572872 | tf_op jit(solution)/shard_map/ppermute | solution.py:337
  166.3 0.0 collective-permute-done.17.rest_7_
  166.3 0.8 copy-done.2
  167.1 0.0 collective-permute-start.5
  167.1 0.1 select_reduce_fusion
  167.3 0.8 concatenate.7.table_ref
  168.0 1.0 copy-done.3
  169.1 13.9 %correlate_tiles.2.rest_8_ = f32[2,8,5,256,256]{4,3,2,1,0:T(8,128)} custom-call(s32[19]{0:T(128)S(1)} %concatenate.7.table_ref, bf16[4,2,4,32,256]{4,3,2,1,0:T(8,128)(2,1)S(1)} %all_to_all.21.rest_0_, bf16[4,2,4,32,256]{4,3,2,1,0:T(8,128)(2,1)} %collective-permute-done.12.rest_1_, bf16[4,2,4,32,256]{4,3,2,1,0:T(8,128)(2,1)} %collective-permute-done.13.rest_2_, ...), custom_call_target="tpu_custom_call" | custom-call | flops 2684354560 | bytes 16777216 | tf_op jit(solution)/shard_map/correlate_tiles/pallas_call | solution.py:290
  183.0 0.0 collective-permute-done.9.rest_5_
  183.0 0.0 collective-permute-done.3.rest_1_
  183.0 0.0 collective-permute-done.5.rest_3_
  183.0 13.8 %correlate_tiles.3 = f32[2,8,5,256,256]{4,3,2,1,0:T(8,128)} custom-call(s32[19]{0:T(128)S(1)} %concatenate.7.table_ref, bf16[4,2,4,32,256]{4,3,2,1,0:T(8,128)(2,1)S(1)} %all-to-all-done.rest_0_, bf16[4,2,4,32,256]{4,3,2,1,0:T(8,128)(2,1)} %collective-permute-done.3.rest_1_, ...), custom_call_target="tpu_custom_call", output_to_operand_aliasing={{}: (9, {})} | custom-call | flops 2684354560 | bytes 16777216 | tf_op jit(solution)/shard_map/correlate_tiles/pallas_call | solution.py:290
  (26 shorter events, 0.1 us)
Async XLA Ops:
  0.0 136.2 %copy-start.10 = (s32[10,10]{1,0:T(8,128)S(1)}, s32[10,10]{1,0:T(8,128)}, u32[]{:S(2)}) copy-start(s32[10,10]{1,0:T(8,128)} %constant.50.clone) | copy-start | bytes 1204
  0.0 136.3 %copy-start.11 = (pred[10,4]{0,1:T(4,128)(4,1)S(1)}, pred[10,4]{0,1:T(4,128)(4,1)}, u32[]{:S(2)}) copy-start(pred[10,4]{0,1:T(4,128)(4,1)} %constant.54.clone) | copy-start | bytes 124
  0.0 136.3 %copy-start.12 = (pred[10,4]{0,1:T(4,128)(4,1)S(1)}, pred[10,4]{0,1:T(4,128)(4,1)}, u32[]{:S(2)}) copy-start(pred[10,4]{0,1:T(4,128)(4,1)} %constant.53.clone) | copy-start | bytes 124
  0.0 122.3 %copy-start.13 = (s32[10]{0:T(128)S(1)}, s32[10]{0:T(128)}, u32[]{:S(2)}) copy-start(s32[10]{0:T(128)} %param.20) | copy-start | bytes 124
  0.0 136.0 %copy-start.14 = (s32[4]{0:T(128)S(1)}, s32[4]{0:T(128)}, u32[]{:S(2)}) copy-start(s32[4]{0:T(128)} %param.19) | copy-start | bytes 52
  0.1 1.6 copy-start
  3.1 7.2 %collective-permute-start.6 = (bf16[2,32,2048]{2,1,0:T(8,128)(2,1)S(1)}, bf16[2,32,2048]{2,1,0:T(8,128)(2,1)S(1)}, u32[]{:S(2)}, u32[]{:S(2)}) collective-permute-start(bf16[2,32,2048]{2,1,0:T(8,128)(2,1)S(1)} %get-tuple-element.23), channel_id=1, source_target_pairs={{0,4},{4,8},{8,12},{12,0},{1,5},{5,9},{9,13},{13,1},{2,6},{6,10},{... | collective-permute-start | bytes 786440 | tf_op jit(solution)/shard_map/ppermute | solution.py:326
  4.5 21.8 %collective-permute-start.7 = (bf16[2,32,2048]{2,1,0:T(8,128)(2,1)S(1)}, bf16[2,32,2048]{2,1,0:T(8,128)(2,1)S(1)}, u32[]{:S(2)}, u32[]{:S(2)}) collective-permute-start(bf16[2,32,2048]{2,1,0:T(8,128)(2,1)S(1)} %get-tuple-element.24), channel_id=1, source_target_pairs={{0,8},{4,12},{8,0},{12,4},{1,9},{5,13},{9,1},{13,5},{2,10},{6,14},... | collective-permute-start | bytes 786440 | tf_op jit(solution)/shard_map/ppermute | solution.py:326
  5.6 23.6 %collective-permute-start.8 = (bf16[2,32,2048]{2,1,0:T(8,128)(2,1)S(1)}, bf16[2,32,2048]{2,1,0:T(8,128)(2,1)S(1)}, u32[]{:S(2)}, u32[]{:S(2)}) collective-permute-start(bf16[2,32,2048]{2,1,0:T(8,128)(2,1)S(1)} %get-tuple-element.25), channel_id=1, source_target_pairs={{0,12},{4,0},{8,4},{12,8},{1,13},{5,1},{9,5},{13,9},{2,14},{6,2},{... | collective-permute-start | bytes 786440 | tf_op jit(solution)/shard_map/ppermute | solution.py:326
  29.2 1.0 copy-start.4
  30.2 1.0 copy-start.6
  31.2 0.7 copy-start.8
  50.2 48.2 %all-to-all-start.3 = ((bf16[4,2,4,32,256]{4,3,2,1,0:T(8,128)(2,1)}), bf16[4,2,4,32,256]{4,3,2,1,0:T(8,128)(2,1)S(1)}, u32[]{:S(2)}, u32[]{:S(2)}) async-start(bf16[4,2,4,32,256]{4,3,2,1,0:T(8,128)(2,1)} %get-tuple-element.28), calls=%async_computation.3 | async-start | bytes 1048576 | tf_op jit(solution)/shard_map/all_to_all | solution.py:406
  55.9 1.6 copy-start.1
  58.9 24.4 %collective-permute-start = (bf16[2,32,2048]{2,1,0:T(8,128)(2,1)S(1)}, bf16[2,32,2048]{2,1,0:T(8,128)(2,1)S(1)}, u32[]{:S(2)}, u32[]{:S(2)}) collective-permute-start(bf16[2,32,2048]{2,1,0:T(8,128)(2,1)S(1)} %get-tuple-element.18), channel_id=1, source_target_pairs={{0,4},{4,8},{8,12},{12,0},{1,5},{5,9},{9,13},{13,1},{2,6},{6,10},{... | collective-permute-start | bytes 786440 | tf_op jit(solution)/shard_map/ppermute | solution.py:326
  60.1 28.7 %collective-permute-start.1 = (bf16[2,32,2048]{2,1,0:T(8,128)(2,1)S(1)}, bf16[2,32,2048]{2,1,0:T(8,128)(2,1)S(1)}, u32[]{:S(2)}, u32[]{:S(2)}) collective-permute-start(bf16[2,32,2048]{2,1,0:T(8,128)(2,1)S(1)} %get-tuple-element.19), channel_id=1, source_target_pairs={{0,8},{4,12},{8,0},{12,4},{1,9},{5,13},{9,1},{13,5},{2,10},{6,14},... | collective-permute-start | bytes 786440 | tf_op jit(solution)/shard_map/ppermute | solution.py:326
  61.1 30.1 %collective-permute-start.2 = (bf16[2,32,2048]{2,1,0:T(8,128)(2,1)S(1)}, bf16[2,32,2048]{2,1,0:T(8,128)(2,1)S(1)}, u32[]{:S(2)}, u32[]{:S(2)}) collective-permute-start(bf16[2,32,2048]{2,1,0:T(8,128)(2,1)S(1)} %get-tuple-element.20), channel_id=1, source_target_pairs={{0,12},{4,0},{8,4},{12,8},{1,13},{5,1},{9,5},{13,9},{2,14},{6,2},{... | collective-permute-start | bytes 786440 | tf_op jit(solution)/shard_map/ppermute | solution.py:326
  91.1 1.0 copy-start.5
  92.2 1.0 copy-start.7
  93.2 0.7 copy-start.9
  112.3 16.6 %all-to-all-start = ((bf16[4,2,4,32,256]{4,3,2,1,0:T(8,128)(2,1)}), bf16[4,2,4,32,256]{4,3,2,1,0:T(8,128)(2,1)S(1)}, u32[]{:S(2)}, u32[]{:S(2)}) async-start(bf16[4,2,4,32,256]{4,3,2,1,0:T(8,128)(2,1)} %get-tuple-element.21), calls=%async_computation | async-start | bytes 1048576 | tf_op jit(solution)/shard_map/all_to_all | solution.py:406
  118.3 11.2 %collective-permute-start.16 = (bf16[4,2,4,32,256]{4,3,2,1,0:T(8,128)(2,1)S(1)}, bf16[4,2,4,32,256]{4,3,2,1,0:T(8,128)(2,1)}, u32[]{:S(2)}, u32[]{:S(2)}) collective-permute-start(bf16[4,2,4,32,256]{4,3,2,1,0:T(8,128)(2,1)S(1)} %all-to-all-done.3.rest_4_), channel_id=1, source_target_pairs={{0,2},{1,3},{2,0},{3,1},{4,6},{5,7},{6,4},{7,5},{8,10},{9,11},{10,... | collective-permute-start | bytes 1572872 | tf_op jit(solution)/shard_map/ppermute | solution.py:337
  118.5 11.3 %collective-permute-start.15 = (bf16[4,2,4,32,256]{4,3,2,1,0:T(8,128)(2,1)S(1)}, bf16[4,2,4,32,256]{4,3,2,1,0:T(8,128)(2,1)}, u32[]{:S(2)}, u32[]{:S(2)}) collective-permute-start(bf16[4,2,4,32,256]{4,3,2,1,0:T(8,128)(2,1)S(1)} %all-to-all-done.3.rest_4_), channel_id=1, source_target_pairs={{0,1},{1,0},{2,3},{3,2},{4,5},{5,4},{6,7},{7,6},{8,9},{9,8},{10,11... | collective-permute-start | bytes 1572872 | tf_op jit(solution)/shard_map/ppermute | solution.py:337
  121.1 19.7 %collective-permute-start.13 = (bf16[4,2,4,32,256]{4,3,2,1,0:T(8,128)(2,1)S(1)}, bf16[4,2,4,32,256]{4,3,2,1,0:T(8,128)(2,1)}, u32[]{:S(2)}, u32[]{:S(2)}) collective-permute-start(bf16[4,2,4,32,256]{4,3,2,1,0:T(8,128)(2,1)S(1)} %all_to_all.21.rest_0_), channel_id=1, source_target_pairs={{0,2},{1,3},{2,0},{3,1},{4,6},{5,7},{6,4},{7,5},{8,10},{9,11},{10,... | collective-permute-start | bytes 1572872 | tf_op jit(solution)/shard_map/ppermute | solution.py:337
  123.0 34.9 %collective-permute-start.12 = (bf16[4,2,4,32,256]{4,3,2,1,0:T(8,128)(2,1)S(1)}, bf16[4,2,4,32,256]{4,3,2,1,0:T(8,128)(2,1)}, u32[]{:S(2)}, u32[]{:S(2)}) collective-permute-start(bf16[4,2,4,32,256]{4,3,2,1,0:T(8,128)(2,1)S(1)} %all_to_all.21.rest_0_), channel_id=1, source_target_pairs={{0,1},{1,0},{2,3},{3,2},{4,5},{5,4},{6,7},{7,6},{8,9},{9,8},{10,11... | collective-permute-start | bytes 1572872 | tf_op jit(solution)/shard_map/ppermute | solution.py:337
  123.3 28.6 %collective-permute-start.10 = (bf16[4,2,4,32,256]{4,3,2,1,0:T(8,128)(2,1)S(1)}, bf16[4,2,4,32,256]{4,3,2,1,0:T(8,128)(2,1)S(1)}, u32[]{:S(2)}, u32[]{:S(2)}) collective-permute-start(bf16[4,2,4,32,256]{4,3,2,1,0:T(8,128)(2,1)S(1)} %all_to_all.20.rest_4_), channel_id=1, source_target_pairs={{0,2},{1,3},{2,0},{3,1},{4,6},{5,7},{6,4},{7,5},{8,10},{9,11},{10,... | collective-permute-start | bytes 1572872 | tf_op jit(solution)/shard_map/ppermute | solution.py:337
  129.5 33.6 %collective-permute-start.4 = (bf16[4,2,4,32,256]{4,3,2,1,0:T(8,128)(2,1)S(1)}, bf16[4,2,4,32,256]{4,3,2,1,0:T(8,128)(2,1)S(1)}, u32[]{:S(2)}, u32[]{:S(2)}) collective-permute-start(bf16[4,2,4,32,256]{4,3,2,1,0:T(8,128)(2,1)S(1)} %all-to-all-done.rest_0_), channel_id=1, source_target_pairs={{0,2},{1,3},{2,0},{3,1},{4,6},{5,7},{6,4},{7,5},{8,10},{9,11},{10,... | collective-permute-start | bytes 1572872 | tf_op jit(solution)/shard_map/ppermute | solution.py:337
  129.8 36.5 %collective-permute-start.17 = (bf16[4,2,4,32,256]{4,3,2,1,0:T(8,128)(2,1)}, bf16[4,2,4,32,256]{4,3,2,1,0:T(8,128)(2,1)S(1)}, u32[]{:S(2)}, u32[]{:S(2)}) collective-permute-start(bf16[4,2,4,32,256]{4,3,2,1,0:T(8,128)(2,1)} %collective-permute-done.16.rest_6_), channel_id=1, source_target_pairs={{0,1},{1,0},{2,3},{3,2},{4,5},{5,4},{6,7},{7,6},{8,9},{9,8},{10,11... | collective-permute-start | bytes 1572872 | tf_op jit(solution)/shard_map/ppermute | solution.py:337
  140.8 27.3 %collective-permute-start.14 = (bf16[4,2,4,32,256]{4,3,2,1,0:T(8,128)(2,1)}, bf16[4,2,4,32,256]{4,3,2,1,0:T(8,128)(2,1)}, u32[]{:S(2)}, u32[]{:S(2)}) collective-permute-start(bf16[4,2,4,32,256]{4,3,2,1,0:T(8,128)(2,1)} %collective-permute-done.13.rest_2_), channel_id=1, source_target_pairs={{0,1},{1,0},{2,3},{3,2},{4,5},{5,4},{6,7},{7,6},{8,9},{9,8},{10,11... | collective-permute-start | bytes 1572872 | tf_op jit(solution)/shard_map/ppermute | solution.py:337
  151.9 31.1 %collective-permute-start.9 = (bf16[4,2,4,32,256]{4,3,2,1,0:T(8,128)(2,1)S(1)}, bf16[4,2,4,32,256]{4,3,2,1,0:T(8,128)(2,1)}, u32[]{:S(2)}, u32[]{:S(2)}) collective-permute-start(bf16[4,2,4,32,256]{4,3,2,1,0:T(8,128)(2,1)S(1)} %all_to_all.20.rest_4_), channel_id=1, source_target_pairs={{0,1},{1,0},{2,3},{3,2},{4,5},{5,4},{6,7},{7,6},{8,9},{9,8},{10,11... | collective-permute-start | bytes 1572872 | tf_op jit(solution)/shard_map/ppermute | solution.py:337
  157.9 25.1 %collective-permute-start.3 = (bf16[4,2,4,32,256]{4,3,2,1,0:T(8,128)(2,1)S(1)}, bf16[4,2,4,32,256]{4,3,2,1,0:T(8,128)(2,1)}, u32[]{:S(2)}, u32[]{:S(2)}) collective-permute-start(bf16[4,2,4,32,256]{4,3,2,1,0:T(8,128)(2,1)S(1)} %all-to-all-done.rest_0_), channel_id=1, source_target_pairs={{0,1},{1,0},{2,3},{3,2},{4,5},{5,4},{6,7},{7,6},{8,9},{9,8},{10,11... | collective-permute-start | bytes 1572872 | tf_op jit(solution)/shard_map/ppermute | solution.py:337
  163.1 19.9 %collective-permute-start.11 = (bf16[4,2,4,32,256]{4,3,2,1,0:T(8,128)(2,1)S(1)}, bf16[4,2,4,32,256]{4,3,2,1,0:T(8,128)(2,1)}, u32[]{:S(2)}, u32[]{:S(2)}) collective-permute-start(bf16[4,2,4,32,256]{4,3,2,1,0:T(8,128)(2,1)S(1)} %collective-permute-done.10.rest_6_), channel_id=1, source_target_pairs={{0,1},{1,0},{2,3},{3,2},{4,5},{5,4},{6,7},{7,6},{8,9},{9,8},{10,11... | collective-permute-start | bytes 1572872 | tf_op jit(solution)/shard_map/ppermute | solution.py:337
  166.3 0.8 copy-start.2
  167.1 15.9 %collective-permute-start.5 = (bf16[4,2,4,32,256]{4,3,2,1,0:T(8,128)(2,1)S(1)}, bf16[4,2,4,32,256]{4,3,2,1,0:T(8,128)(2,1)}, u32[]{:S(2)}, u32[]{:S(2)}) collective-permute-start(bf16[4,2,4,32,256]{4,3,2,1,0:T(8,128)(2,1)S(1)} %collective-permute-done.4.rest_2_), channel_id=1, source_target_pairs={{0,1},{1,0},{2,3},{3,2},{4,5},{5,4},{6,7},{7,6},{8,9},{9,8},{10,11... | collective-permute-start | bytes 1572872 | tf_op jit(solution)/shard_map/ppermute | solution.py:337
  168.0 1.0 copy-start.3
where the time goes:
time: 198 us; the launch traced here: 197 us
  waiting for transfers between devices  69.9 us (35%)
  starting transfers between devices  45.4 us (23%)
  Pallas kernels  39.3 us (20%)
  blocking collectives  27.7 us (14%)
  local copies, waits for them, and re-layouts  13.1 us (7%)
    ppermute x6, waiting for transfers between devices, spread(): lax.ppermute(pieces[d], 'ft', [(i, (i + d) % count) for i in range(count)])  49.1 us
    all_to_all x2, blocking collectives, per_device_kernels(): lax.all_to_all(parts, 'ft', split_axis=0, concat_axis=0, tiled=True)  27.7 us
    pallas_call x2, Pallas kernels, correlate(): pl.pallas_call(functools.partial(correlate_kernel, chunks, blocks, scale)...  27.7 us
    ppermute x12, starting transfers between devices, gather_blocks(): lax.ppermute(held[r], 'bl', [(i, i ^ bit) for i in range(count)])  26.3 us
    ppermute x12, waiting for transfers between devices, gather_blocks(): lax.ppermute(held[r], 'bl', [(i, i ^ bit) for i in range(count)])  15.4 us
    all_to_all x2, starting transfers between devices, per_device_kernels(): lax.all_to_all(parts, 'ft', split_axis=0, concat_axis=0, tiled=True)  11.7 us
    unnamed x30, local copies, waits for them, and re-layouts  10.6 us
    pallas_call x2, Pallas kernels, transform_chunk(): pl.pallas_call(functools.partial(transform_kernel, radix, dests), grid_sp...  8.79 us
  transfers between devices with their start and end apart: 20, of which 11 were waited for; matrix products, arithmetic and copies ran while one was open for 2% of the time, Pallas kernels for 10%

commit v1 on v0

--- a/solution.py
+++ b/solution.py
@@ -86,35 +86,41 @@
         o_refs[shift][0] = turned[place_ref[shift]]
 
 
-def pack(voltages, place, chunk, dests, radix):
-    _, samples, _ = voltages.shape
+def pack(voltages, place, dests, radix):
+    _, samples, inputs = voltages.shape
+    chunks = inputs // LANES
     rows = LANES // dests
     return pl.pallas_call(
         functools.partial(pack_kernel, radix),
         grid_spec=pltpu.PrefetchScalarGridSpec(
             num_scalar_prefetch=1,
-            grid=(2,),
-            in_specs=[pl.BlockSpec((1, samples, LANES), lambda p, t: (p, 0, chunk))],
-            out_specs=[pl.BlockSpec((1, rows, samples), lambda p, t: (p, 0, 0))] * dests,
+            grid=(2, chunks),
+            in_specs=[pl.BlockSpec((1, samples, LANES), lambda p, h, t: (p, 0, h))],
+            out_specs=[pl.BlockSpec((1, rows, samples), lambda p, h, t: (p, h, 0))] * dests,
             scratch_shapes=[
                 pltpu.VMEM((samples, LANES), jnp.float32),
                 pltpu.VMEM((dests, rows, samples), jnp.bfloat16),
             ],
         ),
-        out_shape=[jax.ShapeDtypeStruct((2, rows, samples), jnp.bfloat16)] * dests,
+        out_shape=[jax.ShapeDtypeStruct((2, chunks * rows, samples), jnp.bfloat16)] * dests,
         compiler_params=pltpu.CompilerParams(vmem_limit_bytes=VMEM_BYTES),
         name="pack_inputs",
     )(place, voltages)
 
 
-def transform_kernel(radix, dests, place_ref, *rest):
+def transform_kernel(radix, dests, units, place_ref, *rest):
     v_refs = rest[:dests]
-    c_ref, gh_ref, gl_ref, tw_ref = rest[dests : dests + 4]
-    out_refs, (held, split, prod) = rest[dests + 4 : -3], rest[-3:]
+    c_ref, tw_ref, gh_any, gl_any = rest[dests : dests + 4]
+    out_refs = rest[dests + 5 : -8]
+    held, split, prod, made, gh_ref, gl_ref, sem_h, sem_l = rest[-8:]
     spectra, _, rows, samples = held.shape
     taps = c_ref.shape[0]
     inner = samples // radix
     group = spectra * rows
+    fetch_h = pltpu.make_async_copy(gh_any, gh_ref, sem_h)
+    fetch_l = pltpu.make_async_copy(gl_any, gl_ref, sem_l)
+    fetch_h.start()
+    fetch_l.start()
     for shift in range(dests):
         held[place_ref[dests + shift]] = v_refs[shift][...]
 
@@ -139,19 +145,28 @@
                     split[at, part * inner : (part + 1) * inner] = high
                     split[at, (2 + part) * inner : (3 + part) * inner] = low
 
-    high = split[:, : 2 * inner]
-    prod[...] = (
-        jnp.dot(high, gh_ref[...], preferred_element_type=jnp.float32)
-        + jnp.dot(high, gl_ref[...], preferred_element_type=jnp.float32)
-        + jnp.dot(split[:, 2 * inner :], gh_ref[...], preferred_element_type=jnp.float32)
-    )
-
-    halves = len(out_refs)
+    fetch_h.wait()
+    fetch_l.wait()
+
+    @pl.loop(0, radix // 2)
+    def _(pair):
+        at = pl.ds(pl.multiple_of(pair * 2 * group, 2 * group), 2 * group)
+        high = split[at, : 2 * inner]
+        low = split[at, 2 * inner :]
+        prod[at, :] = (
+            jnp.dot(high, gh_ref[...], preferred_element_type=jnp.float32)
+            + jnp.dot(high, gl_ref[...], preferred_element_type=jnp.float32)
+            + jnp.dot(low, gh_ref[...], preferred_element_type=jnp.float32)
+        )
+
+    halves = radix // dests
+    lane_cuts = inner // LANES
 
     @pl.loop(0, spectra)
     def _(s):
         for sub in range(0, rows, ROWS16):
-            for lane in range(0, inner, LANES):
+            for cut in range(lane_cuts):
+                lane = cut * LANES
                 parts = []
                 for phase in range(radix):
                     at = pl.ds(pl.multiple_of(phase * group + s * rows + sub, ROWS16), ROWS16)
@@ -166,36 +181,47 @@
                             (yr * cos_here + yi * sin_here, yi * cos_here - yr * sin_here)
                         )
                 for step, pair in enumerate(butterflies(parts)):
+                    unit = step % halves * lane_cuts + cut
                     for part in range(2):
-                        out_refs[step % halves][
-                            step // halves, part, s, sub : sub + ROWS16, lane : lane + LANES
-                        ] = pair[part].astype(jnp.bfloat16)
-
-
-def transform_chunk(blocks, place, coef_table, radix):
+                        made[step // halves, unit, part, s, sub : sub + ROWS16, :] = pair[
+                            part
+                        ].astype(jnp.bfloat16)
+
+    for shift in range(dests):
+        for unit in range(units):
+            out_refs[unit * dests + shift][...] = made[place_ref[shift], unit]
+
+
+def transform_all(blocks, place, coef_table, radix, after):
     dests = len(blocks)
     _, rows, samples = blocks[0].shape
     spectra = dests
     inner = samples // radix
-    halves = radix // dests
+    units = samples // dests // LANES
     g_high, g_low = matrix_tables(inner)
+    anywhere = pl.BlockSpec(memory_space=pl.ANY)
     vmem = pl.BlockSpec(memory_space=pltpu.VMEM)
     total = radix * spectra * rows
-    return pl.pallas_call(
-        functools.partial(transform_kernel, radix, dests),
+    made = pl.pallas_call(
+        functools.partial(transform_kernel, radix, dests, units),
         grid_spec=pltpu.PrefetchScalarGridSpec(
             num_scalar_prefetch=1,
             grid=(),
-            in_specs=[vmem] * (dests + 4),
-            out_specs=[vmem] * halves,
+            in_specs=[vmem] * (dests + 2) + [anywhere] * 3,
+            out_specs=[vmem] * (units * dests),
             scratch_shapes=[
                 pltpu.VMEM((spectra, 2, rows, samples), jnp.bfloat16),
                 pltpu.VMEM((total, 4 * inner), jnp.bfloat16),
                 pltpu.VMEM((total, 2 * inner), jnp.float32),
+                pltpu.VMEM((dests, units, 2, spectra, rows, LANES), jnp.bfloat16),
+                pltpu.VMEM((2 * inner, 2 * inner), jnp.bfloat16),
+                pltpu.VMEM((2 * inner, 2 * inner), jnp.bfloat16),
+                pltpu.SemaphoreType.DMA,
+                pltpu.SemaphoreType.DMA,
             ],
         ),
-        out_shape=[jax.ShapeDtypeStruct((dests, 2, spectra, rows, inner), jnp.bfloat16)]
-        * halves,
+        out_shape=[jax.ShapeDtypeStruct((2, spectra, rows, LANES), jnp.bfloat16)]
+        * (units * dests),
         cost_estimate=pl.CostEstimate(
             flops=3 * 2 * total * 4 * inner * inner, bytes_accessed=6 << 20, transcendentals=0
         ),
@@ -205,44 +231,67 @@
         place,
         *blocks,
         coef_table,
+        twiddle_tables(radix, inner),
         jnp.asarray(g_high),
         jnp.asarray(g_low),
-        twiddle_tables(radix, inner),
-    )
+        after,
+    )
+    return [made[unit * dests : (unit + 1) * dests] for unit in range(units)]
+
+
+def join_kernel(place_ref, *rest):
+    for shift, piece in enumerate(rest[:-1]):
+        rest[-1][place_ref[len(rest) - 1 + shift]] = piece[...]
+
+
+def join(pieces, place):
+    vmem = pl.BlockSpec(memory_space=pltpu.VMEM)
+    return pl.pallas_call(
+        join_kernel,
+        grid_spec=pltpu.PrefetchScalarGridSpec(
+            num_scalar_prefetch=1, grid=(), in_specs=[vmem] * len(pieces), out_specs=vmem
+        ),
+        out_shape=jax.ShapeDtypeStruct((len(pieces), *pieces[0].shape), pieces[0].dtype),
+        compiler_params=pltpu.CompilerParams(vmem_limit_bytes=VMEM_BYTES // 4),
+        name="join_pieces",
+    )(place, *pieces)
 
 
 def correlate_kernel(chunks, blocks, scale, table_ref, *rest):
-    g_refs, o_ref, left = rest[: chunks * blocks], rest[-2], rest[-1]
-    senders, _, spectra, rows, inner = g_refs[0].shape
+    g_refs, o_ref, left = rest[:blocks], rest[-2], rest[-1]
+    senders, _, spectra, rows, lanes = g_refs[0].shape
     slots = o_ref.shape[2]
-    coarse = inner // AVG
-    side = chunks * senders * rows
+    coarse = lanes // AVG
+    side = senders * rows
+    run = rows // chunks
     step = pl.program_id(0)
 
     @pl.when(step == 0)
     def _():
-        for chunk in range(chunks):
-            for block in range(blocks):
-                source = g_refs[chunk * blocks + block]
-
-                @pl.loop(0, senders)
-                def _(shift, chunk=chunk, block=block, source=source):
-                    sender = shift
-                    row = pl.multiple_of((chunk * senders + sender) * rows, rows)
-                    for part in range(2):
-                        pieces = [source[shift, part, s] for s in range(spectra)]
+        for block in range(blocks):
+            source = g_refs[block]
+
+            @pl.loop(0, senders)
+            def _(sender, block=block, source=source):
+                for part in range(2):
+                    for chunk in range(chunks):
+                        row = pl.multiple_of((chunk * senders + sender) * run, run)
+                        pieces = [
+                            source[sender, part, s, chunk * run : (chunk + 1) * run]
+                            for s in range(spectra)
+                        ]
                         for c in range(coarse):
                             line = jnp.concatenate(
                                 [piece[:, c * AVG : (c + 1) * AVG] for piece in pieces], axis=1
                             )
                             width = line.shape[1]
                             left[
-                                c, block, pl.ds(row, rows), part * width : (part + 1) * width
+                                c, block, pl.ds(row, run), part * width : (part + 1) * width
                             ] = line
                             left[
                                 c,
                                 block,
-                                pl.ds(pl.multiple_of(side + row, rows), rows),
+                                pl.ds(pl.multiple_of(side + row, run), run),
                                 (1 - part) * width : (2 - part) * width,
                             ] = -line if part == 0 else line
 
@@ -270,18 +319,17 @@
             o_ref[:, 0, slot] = jnp.zeros((2, side, side), jnp.float32)
 
 
-def correlate(table, gathered, part_index, part_count, slots, vis):
-    chunks, blocks = len(gathered), len(gathered[0])
-    senders, _, spectra, rows, inner = gathered[0][0].shape
-    coarse = inner // AVG
-    side = chunks * senders * rows
+def correlate(table, gathered, unit, units, chunks, slots, vis):
+    blocks = len(gathered)
+    senders, _, spectra, rows, lanes = gathered[0].shape
+    coarse = lanes // AVG
+    side = senders * rows
     scale = 1.0 / (AVG * spectra)
-    parts = [block for chunk in gathered for block in chunk]
     in_specs = [
-        pl.BlockSpec(part.shape, lambda c, t: (0,) * 5, pipeline_mode=pl.Buffered(1))
-        for part in parts
+        pl.BlockSpec(block.shape, lambda c, t: (0,) * 5, pipeline_mode=pl.Buffered(1))
+        for block in gathered
     ]
-    args = [table, *parts]
+    args = [table, *gathered]
     aliases = {}
     if vis is not None:
         in_specs.append(pl.BlockSpec(memory_space=pl.ANY))
@@ -294,19 +342,17 @@
             grid=(coarse,),
             in_specs=in_specs,
             out_specs=pl.BlockSpec(
-                (2, 1, slots, side, side), lambda c, t: (0, part_index * coarse + c, 0, 0, 0)
+                (2, 1, slots, side, side), lambda c, t: (0, unit * coarse + c, 0, 0, 0)
             ),
             scratch_shapes=[
                 pltpu.VMEM((coarse, blocks, 2 * side, 2 * spectra * AVG), jnp.bfloat16)
             ],
         ),
-        out_shape=jax.ShapeDtypeStruct(
-            (2, part_count * coarse, slots, side, side), jnp.float32
-        ),
+        out_shape=jax.ShapeDtypeStruct((2, units * coarse, slots, side, side), jnp.float32),
         input_output_aliases=aliases,
         cost_estimate=pl.CostEstimate(
             flops=coarse * slots * 2 * 4 * side * side * spectra * AVG,
-            bytes_accessed=16 << 20,
+            bytes_accessed=8 << 20,
             transcendentals=0,
         ),
         compiler_params=pltpu.CompilerParams(vmem_limit_bytes=VMEM_BYTES),
@@ -339,7 +385,7 @@
     return [held[r] for r in range(count)]
 
 
-def tile_tables(block_ids, tile_owner, place):
+def tile_tables(block_ids, tile_owner):
     block_count = lax.axis_size("bl")
     tile_count = block_count * (block_count + 1) // 2
     slot_cap = 2 * tile_count // block_count
@@ -362,7 +408,7 @@
     cols = jnp.sum(jnp.where(here, col_shard[None, :], 0), axis=1)
     index = lax.axis_index("bl")
     table = jnp.concatenate(
-        [rows ^ index, cols ^ index, jnp.sum(mine, keepdims=True), place]
+        [rows ^ index, cols ^ index, jnp.sum(mine, keepdims=True)]
     ).astype(jnp.int32)
     return table, slot_cap
 
@@ -392,22 +438,20 @@
     dests = lax.axis_size("ft")
     taps, chan_count = coefs.shape
     radix = chan_count // MXU
-    chunk_count = voltages.shape[2] // LANES
-    halves = radix // dests
+    chunks = voltages.shape[2] // LANES
     coef_table = coefs.reshape(taps, MXU, radix).transpose(0, 2, 1)
     place = places(dests)
-    table, slot_cap = tile_tables(block_ids, tile_owner, place)
-    arrived = [
-        spread(pack(voltages, place, chunk, dests, radix)) for chunk in range(chunk_count)
-    ]
-    gathered = [[] for _ in range(halves)]
-    for chunk in range(chunk_count):
-        for half, parts in enumerate(transform_chunk(arrived[chunk], place, coef_table, radix)):
-            turned = lax.all_to_all(parts, "ft", split_axis=0, concat_axis=0, tiled=True)
-            gathered[half].append(gather_blocks(turned))
+    table, slot_cap = tile_tables(block_ids, tile_owner)
+    arrived = spread(pack(voltages, place, dests, radix))
+    made = transform_all(arrived, place, coef_table, radix, table)
+    joined = []
+    for unit, parts in enumerate(made):
+        if unit > 1:
+            parts, joined[unit - 2] = lax.optimization_barrier((parts, joined[unit - 2]))
+        joined.append(join(spread(parts), place))
     vis = None
-    for half in range(halves):
-        vis = correlate(table, gathered[half], half, halves, slot_cap, vis)
+    for unit, own in enumerate(joined):
+        vis = correlate(table, gather_blocks(own), unit, len(made), chunks, slot_cap, vis)
     return vis
 
 

time: 198 us -> 176 us (0.89)
  the two profiles are of different devices: /device:TPU:15 before, /device:TPU:21 now
where the time goes in v1:
time: 176 us
  waiting for transfers between devices  82.8 us (47%)
  Pallas kernels  41 us (23%)
  starting transfers between devices  39 us (22%)
  local copies, waits for them, and re-layouts  8.31 us (5%)
  other arithmetic  4.61 us (3%)
    ppermute x15, waiting for transfers between devices, spread(): lax.ppermute(pieces[d], 'ft', [(i, (i + d) % count) for i in range(count)])  66 us
    pallas_call x4, Pallas kernels, correlate(): pl.pallas_call(functools.partial(correlate_kernel, chunks, blocks, scale)...  28.5 us
    ppermute x12, starting transfers between devices, gather_blocks(): lax.ppermute(held[r], 'bl', [(i, i ^ bit) for i in range(count)])  20.9 us
    ppermute x15, starting transfers between devices, spread(): lax.ppermute(pieces[d], 'ft', [(i, (i + d) % count) for i in range(count)])  18.1 us
    ppermute x12, waiting for transfers between devices, gather_blocks(): lax.ppermute(held[r], 'bl', [(i, i ^ bit) for i in range(count)])  16.8 us
    pallas_call x1, Pallas kernels, transform_all(): pl.pallas_call(functools.partial(transform_kernel, radix, dests, units),...  7.05 us
    unnamed x8, local copies, waits for them, and re-layouts  4.39 us
    reshape x2, local copies, waits for them, and re-layouts, per_device_kernels(): coef_table = coefs.reshape(taps, MXU, radix).transpose(0, 2, 1)  3.92 us
  transfers between devices with their start and end apart: 27, of which 14 were waited for; matrix products, arithmetic and copies ran while one was open for 5% of the time, Pallas kernels for 13%

profile of v1, /device:TPU:21, one launch (start us, length us, event | category | flops | bytes accessed | tf_op | source)
XLA Modules:
  0.0 175.8 jit_solution(9458691582610046731)
XLA Ops:
  0.0 0.1 pad_add_fusion.1.place_ref
  0.1 1.6 copy-done
  1.7 3.1 %pack_inputs.1 = (bf16[2,64,2048]{2,1,0:T(8,128)(2,1)S(1)}, bf16[2,64,2048]{2,1,0:T(8,128)(2,1)}, bf16[2,64,2048]{2,1,0:T(8,128)(2,1)S(1)}, bf16[2,64,2048]{2,1,0:T(8,128)(2,1)S(1)}) custom-call(s32[8]{0:T(128)S(1)} %pad_add_fusion.1.place_ref, bf16[2,2048,256]{2,1,0:T(8,128)(2,1)S(1)} %copy-done), custom_call_target="tpu_custom_call" | custom-call | tf_op jit(solution)/shard_map/pack_inputs/pallas_call | solution.py:93
  4.8 1.3 collective-permute-start
  6.1 0.1 collective-permute-start.1
  6.1 1.1 collective-permute-start.2
  7.3 0.8 fusion.1
  8.0 2.4 %reshape.11 = f32[8,256,8]{2,1,0:T(8,128)} reshape(f32[8,2048]{1,0:T(8,128)} %param.15) | data formatting | bytes 131072 | tf_op jit(solution)/shard_map/reshape | solution.py:442
  10.4 1.5 copy.19
  12.0 0.7 broadcast_compare_fusion
  12.6 0.6 reduce_sum.69
  13.3 0.8 select_reduce_fusion.3
  14.0 0.8 multiply_reduce_fusion
  14.8 0.2 select_reduce_fusion.1
  15.0 0.7 pad_add_fusion.rest_8_.table_ref
  15.7 2.2 %collective-permute-done.rest_1_ = bf16[2,64,2048]{2,1,0:T(8,128)(2,1)S(1)} collective-permute-done((bf16[2,64,2048]{2,1,0:T(8,128)(2,1)}, bf16[2,64,2048]{2,1,0:T(8,128)(2,1)S(1)}, u32[]{:S(2)}, u32[]{:S(2)}) %collective-permute-start) | collective-permute-done | bytes 524320 | tf_op jit(solution)/shard_map/ppermute | solution.py:372
  17.9 22.3 %collective-permute-done.1.rest_2_ = bf16[2,64,2048]{2,1,0:T(8,128)(2,1)S(1)} collective-permute-done((bf16[2,64,2048]{2,1,0:T(8,128)(2,1)S(1)}, bf16[2,64,2048]{2,1,0:T(8,128)(2,1)S(1)}, u32[]{:S(2)}, u32[]{:S(2)}) %collective-permute-start.1) | collective-permute-done | bytes 524320 | tf_op jit(solution)/shard_map/ppermute | solution.py:372
  40.2 11.2 %collective-permute-done.2.rest_3_ = bf16[2,64,2048]{2,1,0:T(8,128)(2,1)S(1)} collective-permute-done((bf16[2,64,2048]{2,1,0:T(8,128)(2,1)S(1)}, bf16[2,64,2048]{2,1,0:T(8,128)(2,1)S(1)}, u32[]{:S(2)}, u32[]{:S(2)}) %collective-permute-start.2) | collective-permute-done | bytes 524320 | tf_op jit(solution)/shard_map/ppermute | solution.py:372
  51.4 1.0 copy-done.1
  52.4 1.0 copy-done.2
  53.5 0.7 copy-done.3
  54.2 7.1 %filter_transform.1 = (bf16[2,4,64,128]{3,2,1,0:T(8,128)(2,1)S(1)}, bf16[2,4,64,128]{3,2,1,0:T(8,128)(2,1)S(1)}, bf16[2,4,64,128]{3,2,1,0:T(8,128)(2,1)S(1)}, bf...) custom-call(s32[8]{0:T(128)S(1)} %pad_add_fusion.1.place_ref, ...), custom_call_target="tpu_custom_call" | custom-call | flops 3221225472 | bytes 6291456 | tf_op jit(solution)/shard_map/filter_transform/pallas_call | solution.py:205
  61.3 1.3 collective-permute-start.12
  62.6 2.1 %collective-permute-start.13 = (bf16[2,4,64,128]{3,2,1,0:T(8,128)(2,1)S(1)}, bf16[2,4,64,128]{3,2,1,0:T(8,128)(2,1)S(1)}, u32[]{:S(2)}, u32[]{:S(2)}) collective-permute-start(bf16[2,4,64,128]{3,2,1,0:T(8,128)(2,1)S(1)} %get-tuple-element.57), channel_id=1, source_target_pairs={{0,8},{4,12},{8,0},{12,4},{1,9},{5,13},{9,1},{13,5},{2,10},{6,14},... | collective-permute-start | bytes 393224 | tf_op jit(solution)/shard_map/ppermute | solution.py:372
  64.7 1.5 collective-permute-start.3
  66.2 0.8 collective-permute-done.12.rest_1_
  67.0 4.9 %collective-permute-done.13.rest_2_ = bf16[2,4,64,128]{3,2,1,0:T(8,128)(2,1)S(1)} collective-permute-done((bf16[2,4,64,128]{3,2,1,0:T(8,128)(2,1)S(1)}, bf16[2,4,64,128]{3,2,1,0:T(8,128)(2,1)S(1)}, u32[]{:S(2)}, u32[]{:S(2)}) %collective-permute-start.13) | collective-permute-done | bytes 131104 | tf_op jit(solution)/shard_map/ppermute | solution.py:372
  71.9 5.2 %collective-permute-done.14.rest_3_ = bf16[2,4,64,128]{3,2,1,0:T(8,128)(2,1)S(1)} collective-permute-done((bf16[2,4,64,128]{3,2,1,0:T(8,128)(2,1)S(1)}, bf16[2,4,64,128]{3,2,1,0:T(8,128)(2,1)S(1)}, u32[]{:S(2)}, u32[]{:S(2)}) %collective-permute-start.14) | collective-permute-done | bytes 131104 | tf_op jit(solution)/shard_map/ppermute | solution.py:372
  77.1 0.6 join_pieces.6.rest_0_
  77.7 1.3 collective-permute-start.25
  79.0 0.8 collective-permute-start.24
  79.7 0.0 collective-permute-start.4
  79.7 2.2 %collective-permute-start.5 = (bf16[2,4,64,128]{3,2,1,0:T(8,128)(2,1)S(1)}, bf16[2,4,64,128]{3,2,1,0:T(8,128)(2,1)S(1)}, u32[]{:S(2)}, u32[]{:S(2)}) collective-permute-start(bf16[2,4,64,128]{3,2,1,0:T(8,128)(2,1)S(1)} %get-tuple-element.46), channel_id=1, source_target_pairs={{0,12},{4,0},{8,4},{12,8},{1,13},{5,1},{9,5},{13,9},{2,14},{6,2},{... | collective-permute-start | bytes 393224 | tf_op jit(solution)/shard_map/ppermute | solution.py:372
  81.9 1.2 collective-permute-start.15
  83.1 2.7 %collective-permute-done.4.rest_2_ = bf16[2,4,64,128]{3,2,1,0:T(8,128)(2,1)S(1)} collective-permute-done((bf16[2,4,64,128]{3,2,1,0:T(8,128)(2,1)S(1)}, bf16[2,4,64,128]{3,2,1,0:T(8,128)(2,1)S(1)}, u32[]{:S(2)}, u32[]{:S(2)}) %collective-permute-start.4) | collective-permute-done | bytes 131104 | tf_op jit(solution)/shard_map/ppermute | solution.py:372
  85.8 0.2 collective-permute-start.16
  86.0 3.7 %collective-permute-done.5.rest_3_ = bf16[2,4,64,128]{3,2,1,0:T(8,128)(2,1)S(1)} collective-permute-done((bf16[2,4,64,128]{3,2,1,0:T(8,128)(2,1)S(1)}, bf16[2,4,64,128]{3,2,1,0:T(8,128)(2,1)S(1)}, u32[]{:S(2)}, u32[]{:S(2)}) %collective-permute-start.5) | collective-permute-done | bytes 131104 | tf_op jit(solution)/shard_map/ppermute | solution.py:372
  89.6 4.3 %collective-permute-start.17 = (bf16[2,4,64,128]{3,2,1,0:T(8,128)(2,1)S(1)}, bf16[2,4,64,128]{3,2,1,0:T(8,128)(2,1)S(1)}, u32[]{:S(2)}, u32[]{:S(2)}) collective-permute-start(bf16[2,4,64,128]{3,2,1,0:T(8,128)(2,1)S(1)} %get-tuple-element.62), channel_id=1, source_target_pairs={{0,12},{4,0},{8,4},{12,8},{1,13},{5,1},{9,5},{13,9},{2,14},{6,2},{... | collective-permute-start | bytes 393224 | tf_op jit(solution)/shard_map/ppermute | solution.py:372
  94.0 0.6 join_pieces.4.rest_0_
  94.5 5.4 %collective-permute-done.15.rest_1_ = bf16[2,4,64,128]{3,2,1,0:T(8,128)(2,1)S(1)} collective-permute-done((bf16[2,4,64,128]{3,2,1,0:T(8,128)(2,1)S(1)}, bf16[2,4,64,128]{3,2,1,0:T(8,128)(2,1)S(1)}, u32[]{:S(2)}, u32[]{:S(2)}) %collective-permute-start.15) | collective-permute-done | bytes 131104 | tf_op jit(solution)/shard_map/ppermute | solution.py:372
  99.9 0.3 collective-permute-start.7
  100.2 2.3 %collective-permute-done.17.rest_3_ = bf16[2,4,64,128]{3,2,1,0:T(8,128)(2,1)S(1)} collective-permute-done((bf16[2,4,64,128]{3,2,1,0:T(8,128)(2,1)S(1)}, bf16[2,4,64,128]{3,2,1,0:T(8,128)(2,1)S(1)}, u32[]{:S(2)}, u32[]{:S(2)}) %collective-permute-start.17) | collective-permute-done | bytes 131104 | tf_op jit(solution)/shard_map/ppermute | solution.py:372
  102.5 2.6 %collective-permute-start.8 = (bf16[2,4,64,128]{3,2,1,0:T(8,128)(2,1)S(1)}, bf16[2,4,64,128]{3,2,1,0:T(8,128)(2,1)S(1)}, u32[]{:S(2)}, u32[]{:S(2)}) collective-permute-start(bf16[2,4,64,128]{3,2,1,0:T(8,128)(2,1)S(1)} %get-tuple-element.50), channel_id=1, source_target_pairs={{0,12},{4,0},{8,4},{12,8},{1,13},{5,1},{9,5},{13,9},{2,14},{6,2},{... | collective-permute-start | bytes 393224 | tf_op jit(solution)/shard_map/ppermute | solution.py:372
  105.1 5.4 %collective-permute-done.6.rest_1_ = bf16[2,4,64,128]{3,2,1,0:T(8,128)(2,1)S(1)} collective-permute-done((bf16[2,4,64,128]{3,2,1,0:T(8,128)(2,1)S(1)}, bf16[2,4,64,128]{3,2,1,0:T(8,128)(2,1)S(1)}, u32[]{:S(2)}, u32[]{:S(2)}) %collective-permute-start.6) | collective-permute-done | bytes 131104 | tf_op jit(solution)/shard_map/ppermute | solution.py:372
  110.5 0.3 collective-permute-start.22
  110.7 0.6 join_pieces.7.rest_0_
  111.3 0.0 collective-permute-done.7.rest_2_
  111.3 2.4 %collective-permute-start.21 = (bf16[4,2,4,64,128]{4,3,2,1,0:T(8,128)(2,1)S(1)}, bf16[4,2,4,64,128]{4,3,2,1,0:T(8,128)(2,1)S(1)}, u32[]{:S(2)}, u32[]{:S(2)}) collective-permute-start(bf16[4,2,4,64,128]{4,3,2,1,0:T(8,128)(2,1)S(1)} %join_pieces.4.rest_0_), channel_id=1, source_target_pairs={{0,1},{1,0},{2,3},{3,2},{4,5},{5,4},{6,7},{7,6},{8,9},{9,8},{10,11... | collective-permute-start | bytes 1572872 | tf_op jit(solution)/shard_map/ppermute | solution.py:383
  113.7 1.2 collective-permute-start.19
  115.0 0.6 join_pieces.5.rest_0_
  115.5 0.3 collective-permute-start.10
  115.9 0.6 collective-permute-start.26
  116.5 5.3 %collective-permute-done.22.rest_2_ = bf16[4,2,4,64,128]{4,3,2,1,0:T(8,128)(2,1)S(1)} collective-permute-done((bf16[4,2,4,64,128]{4,3,2,1,0:T(8,128)(2,1)S(1)}, bf16[4,2,4,64,128]{4,3,2,1,0:T(8,128)(2,1)S(1)}, u32[]{:S(2)}, u32[]{:S(2)}) %collective-permute-start.22) | collective-permute-done | bytes 524320 | tf_op jit(solution)/shard_map/ppermute | solution.py:383
  121.9 5.5 %collective-permute-start.23 = (bf16[4,2,4,64,128]{4,3,2,1,0:T(8,128)(2,1)S(1)}, bf16[4,2,4,64,128]{4,3,2,1,0:T(8,128)(2,1)S(1)}, u32[]{:S(2)}, u32[]{:S(2)}) collective-permute-start(bf16[4,2,4,64,128]{4,3,2,1,0:T(8,128)(2,1)S(1)} %collective-permute-done.22.rest_2_), channel_id=1, source_target_pairs={{0,1},{1,0},{2,3},{3,2},{4,5},{5,4},{6,7},{7,6},{8,9},{9,8},{10,11... | collective-permute-start | bytes 1572872 | tf_op jit(solution)/shard_map/ppermute | solution.py:383
  127.4 0.0 collective-permute-start.18
  127.4 5.7 %collective-permute-done.19.rest_2_ = bf16[4,2,4,64,128]{4,3,2,1,0:T(8,128)(2,1)S(1)} collective-permute-done((bf16[4,2,4,64,128]{4,3,2,1,0:T(8,128)(2,1)S(1)}, bf16[4,2,4,64,128]{4,3,2,1,0:T(8,128)(2,1)S(1)}, u32[]{:S(2)}, u32[]{:S(2)}) %collective-permute-start.19) | collective-permute-done | bytes 524320 | tf_op jit(solution)/shard_map/ppermute | solution.py:383
  133.1 5.5 %collective-permute-start.20 = (bf16[4,2,4,64,128]{4,3,2,1,0:T(8,128)(2,1)S(1)}, bf16[4,2,4,64,128]{4,3,2,1,0:T(8,128)(2,1)S(1)}, u32[]{:S(2)}, u32[]{:S(2)}) collective-permute-start(bf16[4,2,4,64,128]{4,3,2,1,0:T(8,128)(2,1)S(1)} %collective-permute-done.19.rest_2_), channel_id=1, source_target_pairs={{0,1},{1,0},{2,3},{3,2},{4,5},{5,4},{6,7},{7,6},{8,9},{9,8},{10,11... | collective-permute-start | bytes 1572872 | tf_op jit(solution)/shard_map/ppermute | solution.py:383
  138.6 5.7 %collective-permute-done.10.rest_2_ = bf16[4,2,4,64,128]{4,3,2,1,0:T(8,128)(2,1)S(1)} collective-permute-done((bf16[4,2,4,64,128]{4,3,2,1,0:T(8,128)(2,1)S(1)}, bf16[4,2,4,64,128]{4,3,2,1,0:T(8,128)(2,1)S(1)}, u32[]{:S(2)}, u32[]{:S(2)}) %collective-permute-start.10) | collective-permute-done | bytes 524320 | tf_op jit(solution)/shard_map/ppermute | solution.py:383
  144.3 3.0 %collective-permute-start.9 = (bf16[4,2,4,64,128]{4,3,2,1,0:T(8,128)(2,1)S(1)}, bf16[4,2,4,64,128]{4,3,2,1,0:T(8,128)(2,1)S(1)}, u32[]{:S(2)}, u32[]{:S(2)}) collective-permute-start(bf16[4,2,4,64,128]{4,3,2,1,0:T(8,128)(2,1)S(1)} %join_pieces.5.rest_0_), channel_id=1, source_target_pairs={{0,1},{1,0},{2,3},{3,2},{4,5},{5,4},{6,7},{7,6},{8,9},{9,8},{10,11... | collective-permute-start | bytes 1572872 | tf_op jit(solution)/shard_map/ppermute | solution.py:383
  147.3 0.0 collective-permute-start.11
  147.3 7.1 %correlate_tiles.4.rest_4_ = f32[2,8,5,256,256]{4,3,2,1,0:T(8,128)} custom-call(s32[11]{0:T(128)S(1)} %pad_add_fusion.rest_8_.table_ref, bf16[4,2,4,64,128]{4,3,2,1,0:T(8,128)(2,1)S(1)} %join_pieces.6.rest_0_, bf16[4,2,4,64,128]{4,3,2,1,0:T(8,128)(2,1)S(1)} %collective-permute-done.24.rest_1_, ...), custom_call_target="tpu_custom_call" | custom-call | flops 1342177280 | bytes 8388608 | tf_op jit(solution)/shard_map/correlate_tiles/pallas_call | solution.py:338
  154.4 7.1 %correlate_tiles.5.rest_4_ = f32[2,8,5,256,256]{4,3,2,1,0:T(8,128)} custom-call(s32[11]{0:T(128)S(1)} %pad_add_fusion.rest_8_.table_ref, bf16[4,2,4,64,128]{4,3,2,1,0:T(8,128)(2,1)S(1)} %join_pieces.4.rest_0_, bf16[4,2,4,64,128]{4,3,2,1,0:T(8,128)(2,1)S(1)} %collective-permute-done.21.rest_1_, ...), custom_call_target="tpu_custom_call", output_to_operand_aliasing={{}: (5, {})} | custom-call | flops 1342177280 | bytes 8388608 | tf_op jit(solution)/shard_map/correlate_tiles/pallas_call | solution.py:338
  161.6 7.1 %correlate_tiles.6.rest_4_ = f32[2,8,5,256,256]{4,3,2,1,0:T(8,128)} custom-call(s32[11]{0:T(128)S(1)} %pad_add_fusion.rest_8_.table_ref, bf16[4,2,4,64,128]{4,3,2,1,0:T(8,128)(2,1)S(1)} %join_pieces.7.rest_0_, bf16[4,2,4,64,128]{4,3,2,1,0:T(8,128)(2,1)S(1)} %collective-permute-done.18.rest_1_, ...), custom_call_target="tpu_custom_call", output_to_operand_aliasing={{}: (5, {})} | custom-call | flops 1342177280 | bytes 8388608 | tf_op jit(solution)/shard_map/correlate_tiles/pallas_call | solution.py:338
  168.7 7.1 %correlate_tiles.7 = f32[2,8,5,256,256]{4,3,2,1,0:T(8,128)} custom-call(s32[11]{0:T(128)S(1)} %pad_add_fusion.rest_8_.table_ref, bf16[4,2,4,64,128]{4,3,2,1,0:T(8,128)(2,1)S(1)} %join_pieces.5.rest_0_, bf16[4,2,4,64,128]{4,3,2,1,0:T(8,128)(2,1)S(1)} %collective-permute-done.9.rest_1_, ...), custom_call_target="tpu_custom_call", output_to_operand_aliasing={{}: (5, {})} | custom-call | flops 1342177280 | bytes 8388608 | tf_op jit(solution)/shard_map/correlate_tiles/pallas_call | solution.py:338
  (20 shorter events, 0.1 us)
Async XLA Ops:
  0.1 1.6 copy-start
  4.8 13.1 %collective-permute-start = (bf16[2,64,2048]{2,1,0:T(8,128)(2,1)}, bf16[2,64,2048]{2,1,0:T(8,128)(2,1)S(1)}, u32[]{:S(2)}, u32[]{:S(2)}) collective-permute-start(bf16[2,64,2048]{2,1,0:T(8,128)(2,1)} %get-tuple-element.36), channel_id=1, source_target_pairs={{0,4},{4,8},{8,12},{12,0},{1,5},{5,9},{9,13},{13,1},{2,6},{6,10},{... | collective-permute-start | bytes 1572872 | tf_op jit(solution)/shard_map/ppermute | solution.py:372
  6.1 34.1 %collective-permute-start.1 = (bf16[2,64,2048]{2,1,0:T(8,128)(2,1)S(1)}, bf16[2,64,2048]{2,1,0:T(8,128)(2,1)S(1)}, u32[]{:S(2)}, u32[]{:S(2)}) collective-permute-start(bf16[2,64,2048]{2,1,0:T(8,128)(2,1)S(1)} %get-tuple-element.37), channel_id=1, source_target_pairs={{0,8},{4,12},{8,0},{12,4},{1,9},{5,13},{9,1},{13,5},{2,10},{6,14},... | collective-permute-start | bytes 1572872 | tf_op jit(solution)/shard_map/ppermute | solution.py:372
  6.1 45.3 %collective-permute-start.2 = (bf16[2,64,2048]{2,1,0:T(8,128)(2,1)S(1)}, bf16[2,64,2048]{2,1,0:T(8,128)(2,1)S(1)}, u32[]{:S(2)}, u32[]{:S(2)}) collective-permute-start(bf16[2,64,2048]{2,1,0:T(8,128)(2,1)S(1)} %get-tuple-element.38), channel_id=1, source_target_pairs={{0,12},{4,0},{8,4},{12,8},{1,13},{5,1},{9,5},{13,9},{2,14},{6,2},{... | collective-permute-start | bytes 1572872 | tf_op jit(solution)/shard_map/ppermute | solution.py:372
  51.4 1.0 copy-start.1
  52.4 1.0 copy-start.2
  53.5 0.7 copy-start.3
  61.3 5.7 %collective-permute-start.12 = (bf16[2,4,64,128]{3,2,1,0:T(8,128)(2,1)S(1)}, bf16[2,4,64,128]{3,2,1,0:T(8,128)(2,1)S(1)}, u32[]{:S(2)}, u32[]{:S(2)}) collective-permute-start(bf16[2,4,64,128]{3,2,1,0:T(8,128)(2,1)S(1)} %get-tuple-element.56), channel_id=1, source_target_pairs={{0,4},{4,8},{8,12},{12,0},{1,5},{5,9},{9,13},{13,1},{2,6},{6,10},{... | collective-permute-start | bytes 393224 | tf_op jit(solution)/shard_map/ppermute | solution.py:372
  62.6 9.3 %collective-permute-start.13 = (bf16[2,4,64,128]{3,2,1,0:T(8,128)(2,1)S(1)}, bf16[2,4,64,128]{3,2,1,0:T(8,128)(2,1)S(1)}, u32[]{:S(2)}, u32[]{:S(2)}) collective-permute-start(bf16[2,4,64,128]{3,2,1,0:T(8,128)(2,1)S(1)} %get-tuple-element.57), channel_id=1, source_target_pairs={{0,8},{4,12},{8,0},{12,4},{1,9},{5,13},{9,1},{13,5},{2,10},{6,14},... | collective-permute-start | bytes 393224 | tf_op jit(solution)/shard_map/ppermute | solution.py:372
  64.7 12.4 %collective-permute-start.14 = (bf16[2,4,64,128]{3,2,1,0:T(8,128)(2,1)S(1)}, bf16[2,4,64,128]{3,2,1,0:T(8,128)(2,1)S(1)}, u32[]{:S(2)}, u32[]{:S(2)}) collective-permute-start(bf16[2,4,64,128]{3,2,1,0:T(8,128)(2,1)S(1)} %get-tuple-element.58), channel_id=1, source_target_pairs={{0,12},{4,0},{8,4},{12,8},{1,13},{5,1},{9,5},{13,9},{2,14},{6,2},{... | collective-permute-start | bytes 393224 | tf_op jit(solution)/shard_map/ppermute | solution.py:372
  64.7 17.2 %collective-permute-start.3 = (bf16[2,4,64,128]{3,2,1,0:T(8,128)(2,1)S(1)}, bf16[2,4,64,128]{3,2,1,0:T(8,128)(2,1)S(1)}, u32[]{:S(2)}, u32[]{:S(2)}) collective-permute-start(bf16[2,4,64,128]{3,2,1,0:T(8,128)(2,1)S(1)} %get-tuple-element.44), channel_id=1, source_target_pairs={{0,4},{4,8},{8,12},{12,0},{1,5},{5,9},{9,13},{13,1},{2,6},{6,10},{... | collective-permute-start | bytes 393224 | tf_op jit(solution)/shard_map/ppermute | solution.py:372
  77.7 37.9 %collective-permute-start.25 = (bf16[4,2,4,64,128]{4,3,2,1,0:T(8,128)(2,1)S(1)}, bf16[4,2,4,64,128]{4,3,2,1,0:T(8,128)(2,1)S(1)}, u32[]{:S(2)}, u32[]{:S(2)}) collective-permute-start(bf16[4,2,4,64,128]{4,3,2,1,0:T(8,128)(2,1)S(1)} %join_pieces.6.rest_0_), channel_id=1, source_target_pairs={{0,2},{1,3},{2,0},{3,1},{4,6},{5,7},{6,4},{7,5},{8,10},{9,11},{10,... | collective-permute-start | bytes 1572872 | tf_op jit(solution)/shard_map/ppermute | solution.py:383
  79.0 36.9 %collective-permute-start.24 = (bf16[4,2,4,64,128]{4,3,2,1,0:T(8,128)(2,1)S(1)}, bf16[4,2,4,64,128]{4,3,2,1,0:T(8,128)(2,1)S(1)}, u32[]{:S(2)}, u32[]{:S(2)}) collective-permute-start(bf16[4,2,4,64,128]{4,3,2,1,0:T(8,128)(2,1)S(1)} %join_pieces.6.rest_0_), channel_id=1, source_target_pairs={{0,1},{1,0},{2,3},{3,2},{4,5},{5,4},{6,7},{7,6},{8,9},{9,8},{10,11... | collective-permute-start | bytes 1572872 | tf_op jit(solution)/shard_map/ppermute | solution.py:383
  79.7 6.1 %collective-permute-start.4 = (bf16[2,4,64,128]{3,2,1,0:T(8,128)(2,1)S(1)}, bf16[2,4,64,128]{3,2,1,0:T(8,128)(2,1)S(1)}, u32[]{:S(2)}, u32[]{:S(2)}) collective-permute-start(bf16[2,4,64,128]{3,2,1,0:T(8,128)(2,1)S(1)} %get-tuple-element.45), channel_id=1, source_target_pairs={{0,8},{4,12},{8,0},{12,4},{1,9},{5,13},{9,1},{13,5},{2,10},{6,14},... | collective-permute-start | bytes 393224 | tf_op jit(solution)/shard_map/ppermute | solution.py:372
  79.7 9.9 %collective-permute-start.5 = (bf16[2,4,64,128]{3,2,1,0:T(8,128)(2,1)S(1)}, bf16[2,4,64,128]{3,2,1,0:T(8,128)(2,1)S(1)}, u32[]{:S(2)}, u32[]{:S(2)}) collective-permute-start(bf16[2,4,64,128]{3,2,1,0:T(8,128)(2,1)S(1)} %get-tuple-element.46), channel_id=1, source_target_pairs={{0,12},{4,0},{8,4},{12,8},{1,13},{5,1},{9,5},{13,9},{2,14},{6,2},{... | collective-permute-start | bytes 393224 | tf_op jit(solution)/shard_map/ppermute | solution.py:372
  81.9 18.0 %collective-permute-start.15 = (bf16[2,4,64,128]{3,2,1,0:T(8,128)(2,1)S(1)}, bf16[2,4,64,128]{3,2,1,0:T(8,128)(2,1)S(1)}, u32[]{:S(2)}, u32[]{:S(2)}) collective-permute-start(bf16[2,4,64,128]{3,2,1,0:T(8,128)(2,1)S(1)} %get-tuple-element.60), channel_id=1, source_target_pairs={{0,4},{4,8},{8,12},{12,0},{1,5},{5,9},{9,13},{13,1},{2,6},{6,10},{... | collective-permute-start | bytes 393224 | tf_op jit(solution)/shard_map/ppermute | solution.py:372
  85.8 14.1 %collective-permute-start.16 = (bf16[2,4,64,128]{3,2,1,0:T(8,128)(2,1)S(1)}, bf16[2,4,64,128]{3,2,1,0:T(8,128)(2,1)S(1)}, u32[]{:S(2)}, u32[]{:S(2)}) collective-permute-start(bf16[2,4,64,128]{3,2,1,0:T(8,128)(2,1)S(1)} %get-tuple-element.61), channel_id=1, source_target_pairs={{0,8},{4,12},{8,0},{12,4},{1,9},{5,13},{9,1},{13,5},{2,10},{6,14},... | collective-permute-start | bytes 393224 | tf_op jit(solution)/shard_map/ppermute | solution.py:372
  89.6 12.9 %collective-permute-start.17 = (bf16[2,4,64,128]{3,2,1,0:T(8,128)(2,1)S(1)}, bf16[2,4,64,128]{3,2,1,0:T(8,128)(2,1)S(1)}, u32[]{:S(2)}, u32[]{:S(2)}) collective-permute-start(bf16[2,4,64,128]{3,2,1,0:T(8,128)(2,1)S(1)} %get-tuple-element.62), channel_id=1, source_target_pairs={{0,12},{4,0},{8,4},{12,8},{1,13},{5,1},{9,5},{13,9},{2,14},{6,2},{... | collective-permute-start | bytes 393224 | tf_op jit(solution)/shard_map/ppermute | solution.py:372
  99.9 10.6 %collective-permute-start.6 = (bf16[2,4,64,128]{3,2,1,0:T(8,128)(2,1)S(1)}, bf16[2,4,64,128]{3,2,1,0:T(8,128)(2,1)S(1)}, u32[]{:S(2)}, u32[]{:S(2)}) collective-permute-start(bf16[2,4,64,128]{3,2,1,0:T(8,128)(2,1)S(1)} %get-tuple-element.48), channel_id=1, source_target_pairs={{0,4},{4,8},{8,12},{12,0},{1,5},{5,9},{9,13},{13,1},{2,6},{6,10},{... | collective-permute-start | bytes 393224 | tf_op jit(solution)/shard_map/ppermute | solution.py:372
  99.9 11.4 %collective-permute-start.7 = (bf16[2,4,64,128]{3,2,1,0:T(8,128)(2,1)S(1)}, bf16[2,4,64,128]{3,2,1,0:T(8,128)(2,1)S(1)}, u32[]{:S(2)}, u32[]{:S(2)}) collective-permute-start(bf16[2,4,64,128]{3,2,1,0:T(8,128)(2,1)S(1)} %get-tuple-element.49), channel_id=1, source_target_pairs={{0,8},{4,12},{8,0},{12,4},{1,9},{5,13},{9,1},{13,5},{2,10},{6,14},... | collective-permute-start | bytes 393224 | tf_op jit(solution)/shard_map/ppermute | solution.py:372
  102.5 11.2 %collective-permute-start.8 = (bf16[2,4,64,128]{3,2,1,0:T(8,128)(2,1)S(1)}, bf16[2,4,64,128]{3,2,1,0:T(8,128)(2,1)S(1)}, u32[]{:S(2)}, u32[]{:S(2)}) collective-permute-start(bf16[2,4,64,128]{3,2,1,0:T(8,128)(2,1)S(1)} %get-tuple-element.50), channel_id=1, source_target_pairs={{0,12},{4,0},{8,4},{12,8},{1,13},{5,1},{9,5},{13,9},{2,14},{6,2},{... | collective-permute-start | bytes 393224 | tf_op jit(solution)/shard_map/ppermute | solution.py:372
  110.5 11.4 %collective-permute-start.22 = (bf16[4,2,4,64,128]{4,3,2,1,0:T(8,128)(2,1)S(1)}, bf16[4,2,4,64,128]{4,3,2,1,0:T(8,128)(2,1)S(1)}, u32[]{:S(2)}, u32[]{:S(2)}) collective-permute-start(bf16[4,2,4,64,128]{4,3,2,1,0:T(8,128)(2,1)S(1)} %join_pieces.4.rest_0_), channel_id=1, source_target_pairs={{0,2},{1,3},{2,0},{3,1},{4,6},{5,7},{6,4},{7,5},{8,10},{9,11},{10,... | collective-permute-start | bytes 1572872 | tf_op jit(solution)/shard_map/ppermute | solution.py:383
  111.3 16.1 %collective-permute-start.21 = (bf16[4,2,4,64,128]{4,3,2,1,0:T(8,128)(2,1)S(1)}, bf16[4,2,4,64,128]{4,3,2,1,0:T(8,128)(2,1)S(1)}, u32[]{:S(2)}, u32[]{:S(2)}) collective-permute-start(bf16[4,2,4,64,128]{4,3,2,1,0:T(8,128)(2,1)S(1)} %join_pieces.4.rest_0_), channel_id=1, source_target_pairs={{0,1},{1,0},{2,3},{3,2},{4,5},{5,4},{6,7},{7,6},{8,9},{9,8},{10,11... | collective-permute-start | bytes 1572872 | tf_op jit(solution)/shard_map/ppermute | solution.py:383
  113.7 19.4 %collective-permute-start.19 = (bf16[4,2,4,64,128]{4,3,2,1,0:T(8,128)(2,1)S(1)}, bf16[4,2,4,64,128]{4,3,2,1,0:T(8,128)(2,1)S(1)}, u32[]{:S(2)}, u32[]{:S(2)}) collective-permute-start(bf16[4,2,4,64,128]{4,3,2,1,0:T(8,128)(2,1)S(1)} %join_pieces.7.rest_0_), channel_id=1, source_target_pairs={{0,2},{1,3},{2,0},{3,1},{4,6},{5,7},{6,4},{7,5},{8,10},{9,11},{10,... | collective-permute-start | bytes 1572872 | tf_op jit(solution)/shard_map/ppermute | solution.py:383
  115.5 28.8 %collective-permute-start.10 = (bf16[4,2,4,64,128]{4,3,2,1,0:T(8,128)(2,1)S(1)}, bf16[4,2,4,64,128]{4,3,2,1,0:T(8,128)(2,1)S(1)}, u32[]{:S(2)}, u32[]{:S(2)}) collective-permute-start(bf16[4,2,4,64,128]{4,3,2,1,0:T(8,128)(2,1)S(1)} %join_pieces.5.rest_0_), channel_id=1, source_target_pairs={{0,2},{1,3},{2,0},{3,1},{4,6},{5,7},{6,4},{7,5},{8,10},{9,11},{10,... | collective-permute-start | bytes 1572872 | tf_op jit(solution)/shard_map/ppermute | solution.py:383
  115.9 31.4 %collective-permute-start.26 = (bf16[4,2,4,64,128]{4,3,2,1,0:T(8,128)(2,1)S(1)}, bf16[4,2,4,64,128]{4,3,2,1,0:T(8,128)(2,1)S(1)}, u32[]{:S(2)}, u32[]{:S(2)}) collective-permute-start(bf16[4,2,4,64,128]{4,3,2,1,0:T(8,128)(2,1)S(1)} %collective-permute-done.25.rest_2_), channel_id=1, source_target_pairs={{0,1},{1,0},{2,3},{3,2},{4,5},{5,4},{6,7},{7,6},{8,9},{9,8},{10,11... | collective-permute-start | bytes 1572872 | tf_op jit(solution)/shard_map/ppermute | solution.py:383
  121.9 32.6 %collective-permute-start.23 = (bf16[4,2,4,64,128]{4,3,2,1,0:T(8,128)(2,1)S(1)}, bf16[4,2,4,64,128]{4,3,2,1,0:T(8,128)(2,1)S(1)}, u32[]{:S(2)}, u32[]{:S(2)}) collective-permute-start(bf16[4,2,4,64,128]{4,3,2,1,0:T(8,128)(2,1)S(1)} %collective-permute-done.22.rest_2_), channel_id=1, source_target_pairs={{0,1},{1,0},{2,3},{3,2},{4,5},{5,4},{6,7},{7,6},{8,9},{9,8},{10,11... | collective-permute-start | bytes 1572872 | tf_op jit(solution)/shard_map/ppermute | solution.py:383
  127.4 34.2 %collective-permute-start.18 = (bf16[4,2,4,64,128]{4,3,2,1,0:T(8,128)(2,1)S(1)}, bf16[4,2,4,64,128]{4,3,2,1,0:T(8,128)(2,1)S(1)}, u32[]{:S(2)}, u32[]{:S(2)}) collective-permute-start(bf16[4,2,4,64,128]{4,3,2,1,0:T(8,128)(2,1)S(1)} %join_pieces.7.rest_0_), channel_id=1, source_target_pairs={{0,1},{1,0},{2,3},{3,2},{4,5},{5,4},{6,7},{7,6},{8,9},{9,8},{10,11... | collective-permute-start | bytes 1572872 | tf_op jit(solution)/shard_map/ppermute | solution.py:383
  133.1 28.5 %collective-permute-start.20 = (bf16[4,2,4,64,128]{4,3,2,1,0:T(8,128)(2,1)S(1)}, bf16[4,2,4,64,128]{4,3,2,1,0:T(8,128)(2,1)S(1)}, u32[]{:S(2)}, u32[]{:S(2)}) collective-permute-start(bf16[4,2,4,64,128]{4,3,2,1,0:T(8,128)(2,1)S(1)} %collective-permute-done.19.rest_2_), channel_id=1, source_target_pairs={{0,1},{1,0},{2,3},{3,2},{4,5},{5,4},{6,7},{7,6},{8,9},{9,8},{10,11... | collective-permute-start | bytes 1572872 | tf_op jit(solution)/shard_map/ppermute | solution.py:383
  144.3 24.4 %collective-permute-start.9 = (bf16[4,2,4,64,128]{4,3,2,1,0:T(8,128)(2,1)S(1)}, bf16[4,2,4,64,128]{4,3,2,1,0:T(8,128)(2,1)S(1)}, u32[]{:S(2)}, u32[]{:S(2)}) collective-permute-start(bf16[4,2,4,64,128]{4,3,2,1,0:T(8,128)(2,1)S(1)} %join_pieces.5.rest_0_), channel_id=1, source_target_pairs={{0,1},{1,0},{2,3},{3,2},{4,5},{5,4},{6,7},{7,6},{8,9},{9,8},{10,11... | collective-permute-start | bytes 1572872 | tf_op jit(solution)/shard_map/ppermute | solution.py:383
  147.3 21.4 %collective-permute-start.11 = (bf16[4,2,4,64,128]{4,3,2,1,0:T(8,128)(2,1)S(1)}, bf16[4,2,4,64,128]{4,3,2,1,0:T(8,128)(2,1)S(1)}, u32[]{:S(2)}, u32[]{:S(2)}) collective-permute-start(bf16[4,2,4,64,128]{4,3,2,1,0:T(8,128)(2,1)S(1)} %collective-permute-done.10.rest_2_), channel_id=1, source_target_pairs={{0,1},{1,0},{2,3},{3,2},{4,5},{5,4},{6,7},{7,6},{8,9},{9,8},{10,11... | collective-permute-start | bytes 1572872 | tf_op jit(solution)/shard_map/ppermute | solution.py:383

commit v2 on v1

--- a/solution.py
+++ b/solution.py
@@ -108,19 +108,33 @@
     )(place, voltages)
 
 
+def stage_kernel(*refs):
+    half = len(refs) // 2
+    for source, target in zip(refs[:half], refs[half:]):
+        target[...] = source[...]
+
+
+def stage(*tables):
+    vmem = pl.BlockSpec(memory_space=pltpu.VMEM)
+    return pl.pallas_call(
+        stage_kernel,
+        in_specs=[vmem] * len(tables),
+        out_specs=[vmem] * len(tables),
+        out_shape=[jax.ShapeDtypeStruct(table.shape, table.dtype) for table in tables],
+        compiler_params=pltpu.CompilerParams(vmem_limit_bytes=VMEM_BYTES // 4),
+        name="stage_tables",
+    )(*tables)
+
+
 def transform_kernel(radix, dests, units, place_ref, *rest):
     v_refs = rest[:dests]
-    c_ref, tw_ref, gh_any, gl_any = rest[dests : dests + 4]
-    out_refs = rest[dests + 5 : -8]
-    held, split, prod, made, gh_ref, gl_ref, sem_h, sem_l = rest[-8:]
+    c_ref, tw_ref, gh_ref, gl_ref = rest[dests : dests + 4]
+    out_refs = rest[dests + 5 : -4]
+    held, split, prod, made = rest[-4:]
     spectra, _, rows, samples = held.shape
     taps = c_ref.shape[0]
     inner = samples // radix
     group = spectra * rows
-    fetch_h = pltpu.make_async_copy(gh_any, gh_ref, sem_h)
-    fetch_l = pltpu.make_async_copy(gl_any, gl_ref, sem_l)
-    fetch_h.start()
-    fetch_l.start()
     for shift in range(dests):
         held[place_ref[dests + shift]] = v_refs[shift][...]
 
@@ -144,9 +158,6 @@
                     at = pl.ds(pl.multiple_of(row0 + s * rows + sub, ROWS16), ROWS16)
                     split[at, part * inner : (part + 1) * inner] = high
                     split[at, (2 + part) * inner : (3 + part) * inner] = low
-
-    fetch_h.wait()
-    fetch_l.wait()
 
     @pl.loop(0, radix // 2)
     def _(pair):
@@ -192,13 +203,12 @@
             out_refs[unit * dests + shift][...] = made[place_ref[shift], unit]
 
 
-def transform_all(blocks, place, coef_table, radix, after):
+def transform_all(blocks, place, tables, radix, after):
     dests = len(blocks)
     _, rows, samples = blocks[0].shape
     spectra = dests
     inner = samples // radix
     units = samples // dests // LANES
-    g_high, g_low = matrix_tables(inner)
     anywhere = pl.BlockSpec(memory_space=pl.ANY)
     vmem = pl.BlockSpec(memory_space=pltpu.VMEM)
     total = radix * spectra * rows
@@ -207,17 +217,13 @@
         grid_spec=pltpu.PrefetchScalarGridSpec(
             num_scalar_prefetch=1,
             grid=(),
-            in_specs=[vmem] * (dests + 2) + [anywhere] * 3,
+            in_specs=[vmem] * (dests + 4) + [anywhere],
             out_specs=[vmem] * (units * dests),
             scratch_shapes=[
                 pltpu.VMEM((spectra, 2, rows, samples), jnp.bfloat16),
                 pltpu.VMEM((total, 4 * inner), jnp.bfloat16),
                 pltpu.VMEM((total, 2 * inner), jnp.float32),
                 pltpu.VMEM((dests, units, 2, spectra, rows, LANES), jnp.bfloat16),
-                pltpu.VMEM((2 * inner, 2 * inner), jnp.bfloat16),
-                pltpu.VMEM((2 * inner, 2 * inner), jnp.bfloat16),
-                pltpu.SemaphoreType.DMA,
-                pltpu.SemaphoreType.DMA,
             ],
         ),
         out_shape=[jax.ShapeDtypeStruct((2, spectra, rows, LANES), jnp.bfloat16)]
@@ -230,36 +236,38 @@
     )(
         place,
         *blocks,
-        coef_table,
-        twiddle_tables(radix, inner),
-        jnp.asarray(g_high),
-        jnp.asarray(g_low),
+        *tables,
         after,
     )
     return [made[unit * dests : (unit + 1) * dests] for unit in range(units)]
 
 
-def join_kernel(place_ref, *rest):
-    for shift, piece in enumerate(rest[:-1]):
-        rest[-1][place_ref[len(rest) - 1 + shift]] = piece[...]
-
-
-def join(pieces, place):
+def join_kernel(count, where, place_ref, *rest):
+    for shift in range(count):
+        rest[-1][place_ref[where + shift]] = rest[shift][...]
+
+
+def join(pieces, place, where, after):
     vmem = pl.BlockSpec(memory_space=pltpu.VMEM)
     return pl.pallas_call(
-        join_kernel,
+        functools.partial(join_kernel, len(pieces), where),
         grid_spec=pltpu.PrefetchScalarGridSpec(
-            num_scalar_prefetch=1, grid=(), in_specs=[vmem] * len(pieces), out_specs=vmem
+            num_scalar_prefetch=1,
+            grid=(),
+            in_specs=[vmem] * len(pieces) + [pl.BlockSpec(memory_space=pl.ANY)],
+            out_specs=vmem,
         ),
         out_shape=jax.ShapeDtypeStruct((len(pieces), *pieces[0].shape), pieces[0].dtype),
         compiler_params=pltpu.CompilerParams(vmem_limit_bytes=VMEM_BYTES // 4),
         name="join_pieces",
-    )(place, *pieces)
-
-
-def correlate_kernel(chunks, blocks, scale, table_ref, *rest):
-    g_refs, o_ref, left = rest[:blocks], rest[-2], rest[-1]
-    senders, _, spectra, rows, lanes = g_refs[0].shape
+    )(place, *pieces, after)
+
+
+def correlate_kernel(chunks, scale, table_ref, *rest):
+    o_ref, token_ref, left = rest[-3:]
+    half, senders, _, spectra, rows, lanes = rest[0].shape
+    order = block_order(2 * half)
+    blocks = len(order)
     slots = o_ref.shape[2]
     coarse = lanes // AVG
     side = senders * rows
@@ -268,11 +276,11 @@
 
     @pl.when(step == 0)
     def _():
-        for block in range(blocks):
-            source = g_refs[block]
+        token_ref[...] = jnp.zeros_like(token_ref)
+        for at, block in enumerate(order):
 
             @pl.loop(0, senders)
-            def _(sender, block=block, source=source):
+            def _(sender, block=block, source=rest[at // half].at[at % half]):
                 for part in range(2):
                     for chunk in range(chunks):
                         row = pl.multiple_of((chunk * senders + sender) * run, run)
@@ -320,14 +328,16 @@
 
 
 def correlate(table, gathered, unit, units, chunks, slots, vis):
-    blocks = len(gathered)
-    senders, _, spectra, rows, lanes = gathered[0].shape
+    half, senders, _, spectra, rows, lanes = gathered[0].shape
+    blocks = 2 * half
     coarse = lanes // AVG
     side = senders * rows
     scale = 1.0 / (AVG * spectra)
     in_specs = [
-        pl.BlockSpec(block.shape, lambda c, t: (0,) * 5, pipeline_mode=pl.Buffered(1))
-        for block in gathered
+        pl.BlockSpec(
+            part.shape, lambda c, t, n=part.ndim: (0,) * n, pipeline_mode=pl.Buffered(1)
+        )
+        for part in gathered
     ]
     args = [table, *gathered]
     aliases = {}
@@ -336,19 +346,25 @@
         args.append(vis)
         aliases = {len(args) - 1: 0}
     return pl.pallas_call(
-        functools.partial(correlate_kernel, chunks, blocks, scale),
+        functools.partial(correlate_kernel, chunks, scale),
         grid_spec=pltpu.PrefetchScalarGridSpec(
             num_scalar_prefetch=1,
             grid=(coarse,),
             in_specs=in_specs,
-            out_specs=pl.BlockSpec(
-                (2, 1, slots, side, side), lambda c, t: (0, unit * coarse + c, 0, 0, 0)
-            ),
+            out_specs=[
+                pl.BlockSpec(
+                    (2, 1, slots, side, side), lambda c, t: (0, unit * coarse + c, 0, 0, 0)
+                ),
+                pl.BlockSpec((8, LANES), lambda c, t: (0, 0)),
+            ],
             scratch_shapes=[
                 pltpu.VMEM((coarse, blocks, 2 * side, 2 * spectra * AVG), jnp.bfloat16)
             ],
         ),
-        out_shape=jax.ShapeDtypeStruct((2, units * coarse, slots, side, side), jnp.float32),
+        out_shape=[
+            jax.ShapeDtypeStruct((2, units * coarse, slots, side, side), jnp.float32),
+            jax.ShapeDtypeStruct((8, LANES), jnp.float32),
+        ],
         input_output_aliases=aliases,
         cost_estimate=pl.CostEstimate(
             flops=coarse * slots * 2 * 4 * side * side * spectra * AVG,
@@ -374,15 +390,28 @@
     ]
 
 
-def gather_blocks(own):
+def exchange(own, bit):
     count = lax.axis_size("bl")
-    held = {0: own}
-    bit = count // 2
+    return lax.ppermute(own, "bl", [(i, i ^ bit) for i in range(count)])
+
+
+def gather_blocks(own, partner, after):
+    bit = lax.axis_size("bl") // 2
+    held, other = own[None], partner[None]
+    while bit > 1:
+        both = join([held, other], np.arange(2, dtype=np.int32), 0, after)
+        held = both.reshape(-1, *own.shape)
+        bit //= 2
+        other = exchange(held, bit)
+    return held, other
+
+
+def block_order(count):
+    order, bit = [0], count // 2
     while bit:
-        for r in list(held):
-            held[r ^ bit] = lax.ppermute(held[r], "bl", [(i, i ^ bit) for i in range(count)])
+        order += [r ^ bit for r in order]
         bit //= 2
-    return [held[r] for r in range(count)]
+    return order
 
 
 def tile_tables(block_ids, tile_owner):
@@ -427,6 +456,7 @@
         and radix % dests == 0
         and radix <= 8
         and blocks & (blocks - 1) == 0
+        and blocks > 1
         and inputs % LANES == 0
         and LANES % dests == 0
         and (LANES // dests) % ROWS16 == 0
@@ -442,16 +472,28 @@
     coef_table = coefs.reshape(taps, MXU, radix).transpose(0, 2, 1)
     place = places(dests)
     table, slot_cap = tile_tables(block_ids, tile_owner)
+    tables = stage(coef_table, twiddle_tables(radix, MXU), *matrix_tables(MXU))
     arrived = spread(pack(voltages, place, dests, radix))
-    made = transform_all(arrived, place, coef_table, radix, table)
-    joined = []
-    for unit, parts in enumerate(made):
-        if unit > 1:
-            parts, joined[unit - 2] = lax.optimization_barrier((parts, joined[unit - 2]))
-        joined.append(join(spread(parts), place))
-    vis = None
-    for unit, own in enumerate(joined):
-        vis = correlate(table, gather_blocks(own), unit, len(made), chunks, slot_cap, vis)
+    made = transform_all(arrived, place, tables, radix, table)
+    half = lax.axis_size("bl") // 2
+    partners, tokens, vis = [], [], None
+    for unit in range(len(made) + 1):
+        if unit < len(made):
+            parts = made[unit]
+            if unit > 1:
+                first = (partners[unit - 2][1], arrived)
+                parts, _ = lax.optimization_barrier((parts, first))
+            arrived = spread(parts)
+            own = join(arrived, place, dests, tokens[unit - 2] if unit > 1 else table)
+            partners.append((own, exchange(own, half)))
+        if unit > 0:
+            gathered = gather_blocks(
+                *partners[unit - 1], partners[unit][0] if unit < len(made) else table
+            )
+            vis, token = correlate(
+                table, gathered, unit - 1, len(made), chunks, slot_cap, vis
+            )
+            tokens.append(token)
     return vis
 
 

time: 176 us -> 151 us (0.86)
  the two profiles are of different devices: /device:TPU:21 before, /device:TPU:3 now
where the time goes in v2:
time: 151 us; the launch traced here: 150 us
  waiting for transfers between devices  52 us (34%)
  Pallas kernels  43.5 us (29%)
  starting transfers between devices  41.7 us (28%)
  local copies, waits for them, and re-layouts  8.31 us (6%)
  other arithmetic  4.61 us (3%)
    ppermute x15, waiting for transfers between devices, spread(): lax.ppermute(pieces[d], 'ft', [(i, (i + d) % count) for i in range(count)])  40.9 us
    ppermute x15, starting transfers between devices, spread(): lax.ppermute(pieces[d], 'ft', [(i, (i + d) % count) for i in range(count)])  33.6 us
    pallas_call x4, Pallas kernels, correlate(): pl.pallas_call(functools.partial(correlate_kernel, chunks, scale), grid_s...  28.5 us
    ppermute x8, waiting for transfers between devices, exchange(): return lax.ppermute(own, 'bl', [(i, i ^ bit) for i in range(count)])  11.1 us
    ppermute x8, starting transfers between devices, exchange(): return lax.ppermute(own, 'bl', [(i, i ^ bit) for i in range(count)])  8.07 us
    pallas_call x1, Pallas kernels, transform_all(): pl.pallas_call(functools.partial(transform_kernel, radix, dests, units),...  7.06 us
    pallas_call x8, Pallas kernels, join(): pl.pallas_call(functools.partial(join_kernel, len(pieces), where), grid_s...  4.76 us
    unnamed x8, local copies, waits for them, and re-layouts  4.39 us
  transfers between devices with their start and end apart: 23, of which 9 were waited for; matrix products, arithmetic and copies ran while one was open for 6% of the time, Pallas kernels for 16%

profile of v2, /device:TPU:3, one launch (start us, length us, event | category | flops | bytes accessed | tf_op | source)
XLA Modules:
  0.0 150.3 jit_solution(4603768305677225363)
XLA Ops:
  0.0 0.1 pad_add_fusion.1.place_ref
  0.1 1.6 %copy-done = bf16[2,2048,256]{2,1,0:T(8,128)(2,1)S(1)} copy-done((bf16[2,2048,256]{2,1,0:T(8,128)(2,1)S(1)}, bf16[2,2048,256]{2,1,0:T(8,128)(2,1)}, u32[]{:S(2)}) %copy-start) | copy-done | bytes 2097176
  1.7 3.1 %pack_inputs.1 = (bf16[2,64,2048]{2,1,0:T(8,128)(2,1)S(1)}, bf16[2,64,2048]{2,1,0:T(8,128)(2,1)}, bf16[2,64,2048]{2,1,0:T(8,128)(2,1)S(1)}, bf16[2,64,2048]{2,1,0:T(8,128)(2,1)S(1)}) custom-call(s32[8]{0:T(128)S(1)} %pad_add_fusion.1.place_ref, bf16[2,2048,256]{2,1,0:T(8,128)(2,1)S(1)} %copy-done), custom_call_target="tpu_custom_call" | custom-call | tf_op jit(solution)/shard_map/pack_inputs/pallas_call | solution.py:93
  4.8 1.3 collective-permute-start
  6.1 2.3 %collective-permute-start.1 = (bf16[2,64,2048]{2,1,0:T(8,128)(2,1)S(1)}, bf16[2,64,2048]{2,1,0:T(8,128)(2,1)S(1)}, u32[]{:S(2)}, u32[]{:S(2)}) collective-permute-start(bf16[2,64,2048]{2,1,0:T(8,128)(2,1)S(1)} %get-tuple-element.45), channel_id=1, source_target_pairs={{0,8},{4,12},{8,0},{12,4},{1,9},{5,13},{9,1},{13,5},{2,10},{6,14},... | collective-permute-start | bytes 1572872 | tf_op jit(solution)/shard_map/ppermute | solution.py:388
  8.4 1.1 collective-permute-start.2
  9.5 0.8 fusion.1
  10.2 2.4 %reshape.23 = f32[8,256,8]{2,1,0:T(8,128)} reshape(f32[8,2048]{1,0:T(8,128)} %param.19) | data formatting | bytes 131072 | tf_op jit(solution)/shard_map/reshape | solution.py:472
  12.6 1.5 %copy.23 = f32[8,256,8]{1,2,0:T(8,128)S(1)} copy(f32[8,256,8]{2,1,0:T(8,128)} %reshape.23) | data formatting | bytes 131072 | tf_op jit(solution)/shard_map/reshape | solution.py:472
  14.2 0.7 broadcast_compare_fusion
  14.8 0.6 reduce_sum.69
  15.5 0.8 select_reduce_fusion.3
  16.2 1.0 copy-done.1
  17.3 1.0 copy-done.2
  18.3 0.7 copy-done.3
  19.0 0.1 stage_tables.1
  19.1 0.8 multiply_reduce_fusion
  19.9 0.2 select_reduce_fusion.1
  20.1 0.7 pad_add_fusion.rest_8_.rest_4_.table_ref.rest_2_
  20.8 22.4 %collective-permute-done.1.rest_2_ = bf16[2,64,2048]{2,1,0:T(8,128)(2,1)S(1)} collective-permute-done((bf16[2,64,2048]{2,1,0:T(8,128)(2,1)S(1)}, bf16[2,64,2048]{2,1,0:T(8,128)(2,1)S(1)}, u32[]{:S(2)}, u32[]{:S(2)}) %collective-permute-start.1) | collective-permute-done | bytes 524320 | tf_op jit(solution)/shard_map/ppermute | solution.py:388
  43.2 7.1 %filter_transform.1 = (bf16[2,4,64,128]{3,2,1,0:T(8,128)(2,1)S(1)}, bf16[2,4,64,128]{3,2,1,0:T(8,128)(2,1)S(1)}, bf16[2,4,64,128]{3,2,1,0:T(8,128)(2,1)S(1)}, bf...) custom-call(s32[8]{0:T(128)S(1)} %pad_add_fusion.1.place_ref, ...), custom_call_target="tpu_custom_call" | custom-call | flops 3221225472 | bytes 6291456 | tf_op jit(solution)/shard_map/filter_transform/pallas_call | solution.py:215
  50.3 11.6 %collective-permute-start.7 = (bf16[2,4,64,128]{3,2,1,0:T(8,128)(2,1)S(1)}, bf16[2,4,64,128]{3,2,1,0:T(8,128)(2,1)S(1)}, u32[]{:S(2)}, u32[]{:S(2)}) collective-permute-start(bf16[2,4,64,128]{3,2,1,0:T(8,128)(2,1)S(1)} %get-tuple-element.64), channel_id=1, source_target_pairs={{0,4},{4,8},{8,12},{12,0},{1,5},{5,9},{9,13},{13,1},{2,6},{6,10},{... | collective-permute-start | bytes 393224 | tf_op jit(solution)/shard_map/ppermute | solution.py:388
  61.9 0.3 collective-permute-start.8
  62.1 1.9 %collective-permute-start.9 = (bf16[2,4,64,128]{3,2,1,0:T(8,128)(2,1)S(1)}, bf16[2,4,64,128]{3,2,1,0:T(8,128)(2,1)S(1)}, u32[]{:S(2)}, u32[]{:S(2)}) collective-permute-start(bf16[2,4,64,128]{3,2,1,0:T(8,128)(2,1)S(1)} %get-tuple-element.66), channel_id=1, source_target_pairs={{0,12},{4,0},{8,4},{12,8},{1,13},{5,1},{9,5},{13,9},{2,14},{6,2},{... | collective-permute-start | bytes 393224 | tf_op jit(solution)/shard_map/ppermute | solution.py:388
  64.0 0.2 collective-permute-done.7.rest_1_
  64.2 7.5 %collective-permute-done.8.rest_2_ = bf16[2,4,64,128]{3,2,1,0:T(8,128)(2,1)S(1)} collective-permute-done((bf16[2,4,64,128]{3,2,1,0:T(8,128)(2,1)S(1)}, bf16[2,4,64,128]{3,2,1,0:T(8,128)(2,1)S(1)}, u32[]{:S(2)}, u32[]{:S(2)}) %collective-permute-start.8) | collective-permute-done | bytes 131104 | tf_op jit(solution)/shard_map/ppermute | solution.py:388
  71.7 0.0 collective-permute-done.9.rest_3_
  71.7 0.6 join_pieces.9
  72.3 0.3 collective-permute-start.10
  72.6 3.1 %collective-permute-start.3 = (bf16[2,4,64,128]{3,2,1,0:T(8,128)(2,1)S(1)}, bf16[2,4,64,128]{3,2,1,0:T(8,128)(2,1)S(1)}, u32[]{:S(2)}, u32[]{:S(2)}) collective-permute-start(bf16[2,4,64,128]{3,2,1,0:T(8,128)(2,1)S(1)} %get-tuple-element.56), channel_id=1, source_target_pairs={{0,4},{4,8},{8,12},{12,0},{1,5},{5,9},{9,13},{13,1},{2,6},{6,10},{... | collective-permute-start | bytes 393224 | tf_op jit(solution)/shard_map/ppermute | solution.py:388
  75.7 1.3 collective-permute-start.4
  77.0 0.8 collective-permute-start.5
  77.8 1.2 collective-permute-done.3.rest_1_
  79.1 7.2 %collective-permute-done.4.rest_2_ = bf16[2,4,64,128]{3,2,1,0:T(8,128)(2,1)S(1)} collective-permute-done((bf16[2,4,64,128]{3,2,1,0:T(8,128)(2,1)S(1)}, bf16[2,4,64,128]{3,2,1,0:T(8,128)(2,1)S(1)}, u32[]{:S(2)}, u32[]{:S(2)}) %collective-permute-start.4) | collective-permute-done | bytes 131104 | tf_op jit(solution)/shard_map/ppermute | solution.py:388
  86.3 0.6 join_pieces.8.rest_2_
  86.9 0.0 collective-permute-done.10
  86.9 0.6 join_pieces.10
  87.5 0.8 collective-permute-start.17
  88.3 1.2 collective-permute-start.6
  89.5 2.9 %collective-permute-start.11 = (bf16[2,4,64,128]{3,2,1,0:T(8,128)(2,1)S(1)}, bf16[2,4,64,128]{3,2,1,0:T(8,128)(2,1)S(1)}, u32[]{:S(2)}, u32[]{:S(2)}) collective-permute-start(bf16[2,4,64,128]{3,2,1,0:T(8,128)(2,1)S(1)} %get-tuple-element.68), channel_id=1, source_target_pairs={{0,4},{4,8},{8,12},{12,0},{1,5},{5,9},{9,13},{13,1},{2,6},{6,10},{... | collective-permute-start | bytes 393224 | tf_op jit(solution)/shard_map/ppermute | solution.py:388
  92.4 1.1 collective-permute-start.12
  93.5 1.0 collective-permute-start.13
  94.5 0.0 collective-permute-done.17.rest_1_
  94.5 7.1 %correlate_tiles.4 = (f32[2,8,5,256,256]{4,3,2,1,0:T(8,128)}, f32[8,128]{1,0:T(8,128)S(1)}) custom-call(s32[11]{0:T(128)S(1)} %pad_add_fusion.rest_8_.rest_4_.table_ref.rest_2_, bf16[2,4,2,4,64,128]{5,4,3,2,1,0:T(8,128)(2,1)S(1)} %bitcast.25, bf16[2,4,2,4,64,128]{5,4,3,2,1,0:T(8,128)(2,1)S(1)} %collective-permute-done.17.rest_1_), custom_call_target="tpu_custom_call" | custom-call | flops 1342177280 | bytes 8388608 | tf_op jit(solution)/shard_map/correlate_tiles/pallas_call | solution.py:348
  101.6 1.2 collective-permute-done.12.rest_2_
  102.8 0.6 join_pieces.11.rest_2_
  103.4 0.6 join_pieces.12
  104.0 0.7 collective-permute-start.18
  104.7 3.0 %collective-permute-start.14 = (bf16[2,4,64,128]{3,2,1,0:T(8,128)(2,1)S(1)}, bf16[2,4,64,128]{3,2,1,0:T(8,128)(2,1)S(1)}, u32[]{:S(2)}, u32[]{:S(2)}) collective-permute-start(bf16[2,4,64,128]{3,2,1,0:T(8,128)(2,1)S(1)} %get-tuple-element.72), channel_id=1, source_target_pairs={{0,4},{4,8},{8,12},{12,0},{1,5},{5,9},{9,13},{13,1},{2,6},{6,10},{... | collective-permute-start | bytes 393224 | tf_op jit(solution)/shard_map/ppermute | solution.py:388
  107.7 1.3 collective-permute-start.15
  108.9 0.8 collective-permute-start.16
  109.7 0.3 collective-permute-start.21
  110.0 7.1 %correlate_tiles.5 = (f32[2,8,5,256,256]{4,3,2,1,0:T(8,128)}, f32[8,128]{1,0:T(8,128)S(1)}) custom-call(s32[11]{0:T(128)S(1)} %pad_add_fusion.rest_8_.rest_4_.table_ref.rest_2_, bf16[2,4,2,4,64,128]{5,4,3,2,1,0:T(8,128)(2,1)S(1)} %bitcast.18, bf16[2,4,2,4,64,128]{5,4,3,2,1,0:T(8,128)(2,1)S(1)} %collective-permute-done.18.rest_1_, ...), custom_call_target="tpu_custom_call", output_to_operand_aliasing={{0}: (3, {})} | custom-call | flops 1342177280 | bytes 8388608 | tf_op jit(solution)/shard_map/correlate_tiles/pallas_call | solution.py:348
  117.1 1.1 collective-permute-done.15.rest_2_
  118.2 0.6 join_pieces.13.rest_2_
  118.8 0.3 collective-permute-start.19
  119.1 3.3 %collective-permute-done.21 = bf16[4,2,4,64,128]{4,3,2,1,0:T(8,128)(2,1)S(1)} collective-permute-done((bf16[4,2,4,64,128]{4,3,2,1,0:T(8,128)(2,1)S(1)}, bf16[4,2,4,64,128]{4,3,2,1,0:T(8,128)(2,1)S(1)}, u32[]{:S(2)}, u32[]{:S(2)}) %collective-permute-start.21) | collective-permute-done | bytes 524320 | tf_op jit(solution)/shard_map/ppermute | solution.py:395
  122.5 0.6 join_pieces.15
  123.1 2.9 %collective-permute-start.22 = (bf16[2,4,2,4,64,128]{5,4,3,2,1,0:T(8,128)(2,1)S(1)}, bf16[2,4,2,4,64,128]{5,4,3,2,1,0:T(8,128)(2,1)S(1)}, u32[]{:S(2)}, u32[]{:S(2)}) collective-permute-start(bf16[2,4,2,4,64,128]{5,4,3,2,1,0:T(8,128)(2,1)S(1)} %bitcast.19), channel_id=1, source_target_pairs={{0,1},{1,0},{2,3},{3,2},{4,5},{5,4},{6,7},{7,6},{8,9},{9,8},{10,11... | collective-permute-start | bytes 3145736 | tf_op jit(solution)/shard_map/ppermute | solution.py:395
  126.0 7.8 %collective-permute-done.19 = bf16[4,2,4,64,128]{4,3,2,1,0:T(8,128)(2,1)S(1)} collective-permute-done((bf16[4,2,4,64,128]{4,3,2,1,0:T(8,128)(2,1)S(1)}, bf16[4,2,4,64,128]{4,3,2,1,0:T(8,128)(2,1)S(1)}, u32[]{:S(2)}, u32[]{:S(2)}) %collective-permute-start.19) | collective-permute-done | bytes 524320 | tf_op jit(solution)/shard_map/ppermute | solution.py:395
  133.7 0.6 join_pieces.14
  134.3 1.7 %collective-permute-start.20 = (bf16[2,4,2,4,64,128]{5,4,3,2,1,0:T(8,128)(2,1)S(1)}, bf16[2,4,2,4,64,128]{5,4,3,2,1,0:T(8,128)(2,1)S(1)}, u32[]{:S(2)}, u32[]{:S(2)}) collective-permute-start(bf16[2,4,2,4,64,128]{5,4,3,2,1,0:T(8,128)(2,1)S(1)} %bitcast.21), channel_id=1, source_target_pairs={{0,1},{1,0},{2,3},{3,2},{4,5},{5,4},{6,7},{7,6},{8,9},{9,8},{10,11... | collective-permute-start | bytes 3145736 | tf_op jit(solution)/shard_map/ppermute | solution.py:395
  136.0 7.1 %correlate_tiles.6 = (f32[2,8,5,256,256]{4,3,2,1,0:T(8,128)}, f32[8,128]{1,0:T(8,128)}) custom-call(s32[11]{0:T(128)S(1)} %pad_add_fusion.rest_8_.rest_4_.table_ref.rest_2_, bf16[2,4,2,4,64,128]{5,4,3,2,1,0:T(8,128)(2,1)S(1)} %bitcast.20, bf16[2,4,2,4,64,128]{5,4,3,2,1,0:T(8,128)(2,1)S(1)} %collective-permute-done.22.rest_1_, ...), custom_call_target="tpu_custom_call", output_to_operand_aliasing={{0}: (3, {})} | custom-call | flops 1342177280 | bytes 8388608 | tf_op jit(solution)/shard_map/correlate_tiles/pallas_call | solution.py:348
  143.1 7.1 %correlate_tiles.7 = (f32[2,8,5,256,256]{4,3,2,1,0:T(8,128)}, f32[8,128]{1,0:T(8,128)}) custom-call(s32[11]{0:T(128)S(1)} %pad_add_fusion.rest_8_.rest_4_.table_ref.rest_2_, bf16[2,4,2,4,64,128]{5,4,3,2,1,0:T(8,128)(2,1)S(1)} %bitcast.22, bf16[2,4,2,4,64,128]{5,4,3,2,1,0:T(8,128)(2,1)S(1)} %collective-permute-done.20.rest_1_, ...), custom_call_target="tpu_custom_call", output_to_operand_aliasing={{0}: (3, {})} | custom-call | flops 1342177280 | bytes 8388608 | tf_op jit(solution)/shard_map/correlate_tiles/pallas_call | solution.py:348
  (18 shorter events, 0.1 us)
Async XLA Ops:
  0.1 1.6 %copy-start = (bf16[2,2048,256]{2,1,0:T(8,128)(2,1)S(1)}, bf16[2,2048,256]{2,1,0:T(8,128)(2,1)}, u32[]{:S(2)}) copy-start(bf16[2,2048,256]{2,1,0:T(8,128)(2,1)} %v_ref.1) | copy-start | bytes 6291460
  4.8 16.0 %collective-permute-start = (bf16[2,64,2048]{2,1,0:T(8,128)(2,1)}, bf16[2,64,2048]{2,1,0:T(8,128)(2,1)S(1)}, u32[]{:S(2)}, u32[]{:S(2)}) collective-permute-start(bf16[2,64,2048]{2,1,0:T(8,128)(2,1)} %get-tuple-element.44), channel_id=1, source_target_pairs={{0,4},{4,8},{8,12},{12,0},{1,5},{5,9},{9,13},{13,1},{2,6},{6,10},{... | collective-permute-start | bytes 1572872 | tf_op jit(solution)/shard_map/ppermute | solution.py:388
  6.1 37.1 %collective-permute-start.1 = (bf16[2,64,2048]{2,1,0:T(8,128)(2,1)S(1)}, bf16[2,64,2048]{2,1,0:T(8,128)(2,1)S(1)}, u32[]{:S(2)}, u32[]{:S(2)}) collective-permute-start(bf16[2,64,2048]{2,1,0:T(8,128)(2,1)S(1)} %get-tuple-element.45), channel_id=1, source_target_pairs={{0,8},{4,12},{8,0},{12,4},{1,9},{5,13},{9,1},{13,5},{2,10},{6,14},... | collective-permute-start | bytes 1572872 | tf_op jit(solution)/shard_map/ppermute | solution.py:388
  8.4 34.8 %collective-permute-start.2 = (bf16[2,64,2048]{2,1,0:T(8,128)(2,1)S(1)}, bf16[2,64,2048]{2,1,0:T(8,128)(2,1)S(1)}, u32[]{:S(2)}, u32[]{:S(2)}) collective-permute-start(bf16[2,64,2048]{2,1,0:T(8,128)(2,1)S(1)} %get-tuple-element.46), channel_id=1, source_target_pairs={{0,12},{4,0},{8,4},{12,8},{1,13},{5,1},{9,5},{13,9},{2,14},{6,2},{... | collective-permute-start | bytes 1572872 | tf_op jit(solution)/shard_map/ppermute | solution.py:388
  16.2 1.0 copy-start.1
  17.3 1.0 copy-start.2
  18.3 0.7 copy-start.3
  50.3 13.9 %collective-permute-start.7 = (bf16[2,4,64,128]{3,2,1,0:T(8,128)(2,1)S(1)}, bf16[2,4,64,128]{3,2,1,0:T(8,128)(2,1)S(1)}, u32[]{:S(2)}, u32[]{:S(2)}) collective-permute-start(bf16[2,4,64,128]{3,2,1,0:T(8,128)(2,1)S(1)} %get-tuple-element.64), channel_id=1, source_target_pairs={{0,4},{4,8},{8,12},{12,0},{1,5},{5,9},{9,13},{13,1},{2,6},{6,10},{... | collective-permute-start | bytes 393224 | tf_op jit(solution)/shard_map/ppermute | solution.py:388
  61.9 9.9 %collective-permute-start.8 = (bf16[2,4,64,128]{3,2,1,0:T(8,128)(2,1)S(1)}, bf16[2,4,64,128]{3,2,1,0:T(8,128)(2,1)S(1)}, u32[]{:S(2)}, u32[]{:S(2)}) collective-permute-start(bf16[2,4,64,128]{3,2,1,0:T(8,128)(2,1)S(1)} %get-tuple-element.65), channel_id=1, source_target_pairs={{0,8},{4,12},{8,0},{12,4},{1,9},{5,13},{9,1},{13,5},{2,10},{6,14},... | collective-permute-start | bytes 393224 | tf_op jit(solution)/shard_map/ppermute | solution.py:388
  62.1 9.6 %collective-permute-start.9 = (bf16[2,4,64,128]{3,2,1,0:T(8,128)(2,1)S(1)}, bf16[2,4,64,128]{3,2,1,0:T(8,128)(2,1)S(1)}, u32[]{:S(2)}, u32[]{:S(2)}) collective-permute-start(bf16[2,4,64,128]{3,2,1,0:T(8,128)(2,1)S(1)} %get-tuple-element.66), channel_id=1, source_target_pairs={{0,12},{4,0},{8,4},{12,8},{1,13},{5,1},{9,5},{13,9},{2,14},{6,2},{... | collective-permute-start | bytes 393224 | tf_op jit(solution)/shard_map/ppermute | solution.py:388
  72.3 14.5 %collective-permute-start.10 = (bf16[4,2,4,64,128]{4,3,2,1,0:T(8,128)(2,1)S(1)}, bf16[4,2,4,64,128]{4,3,2,1,0:T(8,128)(2,1)S(1)}, u32[]{:S(2)}, u32[]{:S(2)}) collective-permute-start(bf16[4,2,4,64,128]{4,3,2,1,0:T(8,128)(2,1)S(1)} %join_pieces.9), channel_id=1, source_target_pairs={{0,2},{1,3},{2,0},{3,1},{4,6},{5,7},{6,4},{7,5},{8,10},{9,11},{10,... | collective-permute-start | bytes 1572872 | tf_op jit(solution)/shard_map/ppermute | solution.py:395
  72.6 6.4 %collective-permute-start.3 = (bf16[2,4,64,128]{3,2,1,0:T(8,128)(2,1)S(1)}, bf16[2,4,64,128]{3,2,1,0:T(8,128)(2,1)S(1)}, u32[]{:S(2)}, u32[]{:S(2)}) collective-permute-start(bf16[2,4,64,128]{3,2,1,0:T(8,128)(2,1)S(1)} %get-tuple-element.56), channel_id=1, source_target_pairs={{0,4},{4,8},{8,12},{12,0},{1,5},{5,9},{9,13},{13,1},{2,6},{6,10},{... | collective-permute-start | bytes 393224 | tf_op jit(solution)/shard_map/ppermute | solution.py:388
  75.7 10.5 %collective-permute-start.4 = (bf16[2,4,64,128]{3,2,1,0:T(8,128)(2,1)S(1)}, bf16[2,4,64,128]{3,2,1,0:T(8,128)(2,1)S(1)}, u32[]{:S(2)}, u32[]{:S(2)}) collective-permute-start(bf16[2,4,64,128]{3,2,1,0:T(8,128)(2,1)S(1)} %get-tuple-element.57), channel_id=1, source_target_pairs={{0,8},{4,12},{8,0},{12,4},{1,9},{5,13},{9,1},{13,5},{2,10},{6,14},... | collective-permute-start | bytes 393224 | tf_op jit(solution)/shard_map/ppermute | solution.py:388
  77.0 9.3 %collective-permute-start.5 = (bf16[2,4,64,128]{3,2,1,0:T(8,128)(2,1)S(1)}, bf16[2,4,64,128]{3,2,1,0:T(8,128)(2,1)S(1)}, u32[]{:S(2)}, u32[]{:S(2)}) collective-permute-start(bf16[2,4,64,128]{3,2,1,0:T(8,128)(2,1)S(1)} %get-tuple-element.58), channel_id=1, source_target_pairs={{0,12},{4,0},{8,4},{12,8},{1,13},{5,1},{9,5},{13,9},{2,14},{6,2},{... | collective-permute-start | bytes 393224 | tf_op jit(solution)/shard_map/ppermute | solution.py:388
  87.5 7.0 %collective-permute-start.17 = (bf16[2,4,2,4,64,128]{5,4,3,2,1,0:T(8,128)(2,1)S(1)}, bf16[2,4,2,4,64,128]{5,4,3,2,1,0:T(8,128)(2,1)S(1)}, u32[]{:S(2)}, u32[]{:S(2)}) collective-permute-start(bf16[2,4,2,4,64,128]{5,4,3,2,1,0:T(8,128)(2,1)S(1)} %bitcast.24), channel_id=1, source_target_pairs={{0,1},{1,0},{2,3},{3,2},{4,5},{5,4},{6,7},{7,6},{8,9},{9,8},{10,11... | collective-permute-start | bytes 3145736 | tf_op jit(solution)/shard_map/ppermute | solution.py:395
  88.3 15.1 %collective-permute-start.6 = (bf16[4,2,4,64,128]{4,3,2,1,0:T(8,128)(2,1)S(1)}, bf16[4,2,4,64,128]{4,3,2,1,0:T(8,128)(2,1)S(1)}, u32[]{:S(2)}, u32[]{:S(2)}) collective-permute-start(bf16[4,2,4,64,128]{4,3,2,1,0:T(8,128)(2,1)S(1)} %join_pieces.8.rest_2_), channel_id=1, source_target_pairs={{0,2},{1,3},{2,0},{3,1},{4,6},{5,7},{6,4},{7,5},{8,10},{9,11},{10,... | collective-permute-start | bytes 1572872 | tf_op jit(solution)/shard_map/ppermute | solution.py:395
  89.5 12.1 %collective-permute-start.11 = (bf16[2,4,64,128]{3,2,1,0:T(8,128)(2,1)S(1)}, bf16[2,4,64,128]{3,2,1,0:T(8,128)(2,1)S(1)}, u32[]{:S(2)}, u32[]{:S(2)}) collective-permute-start(bf16[2,4,64,128]{3,2,1,0:T(8,128)(2,1)S(1)} %get-tuple-element.68), channel_id=1, source_target_pairs={{0,4},{4,8},{8,12},{12,0},{1,5},{5,9},{9,13},{13,1},{2,6},{6,10},{... | collective-permute-start | bytes 393224 | tf_op jit(solution)/shard_map/ppermute | solution.py:388
  92.4 10.4 %collective-permute-start.12 = (bf16[2,4,64,128]{3,2,1,0:T(8,128)(2,1)S(1)}, bf16[2,4,64,128]{3,2,1,0:T(8,128)(2,1)S(1)}, u32[]{:S(2)}, u32[]{:S(2)}) collective-permute-start(bf16[2,4,64,128]{3,2,1,0:T(8,128)(2,1)S(1)} %get-tuple-element.69), channel_id=1, source_target_pairs={{0,8},{4,12},{8,0},{12,4},{1,9},{5,13},{9,1},{13,5},{2,10},{6,14},... | collective-permute-start | bytes 393224 | tf_op jit(solution)/shard_map/ppermute | solution.py:388
  93.5 9.3 %collective-permute-start.13 = (bf16[2,4,64,128]{3,2,1,0:T(8,128)(2,1)S(1)}, bf16[2,4,64,128]{3,2,1,0:T(8,128)(2,1)S(1)}, u32[]{:S(2)}, u32[]{:S(2)}) collective-permute-start(bf16[2,4,64,128]{3,2,1,0:T(8,128)(2,1)S(1)} %get-tuple-element.70), channel_id=1, source_target_pairs={{0,12},{4,0},{8,4},{12,8},{1,13},{5,1},{9,5},{13,9},{2,14},{6,2},{... | collective-permute-start | bytes 393224 | tf_op jit(solution)/shard_map/ppermute | solution.py:388
  104.0 6.0 %collective-permute-start.18 = (bf16[2,4,2,4,64,128]{5,4,3,2,1,0:T(8,128)(2,1)S(1)}, bf16[2,4,2,4,64,128]{5,4,3,2,1,0:T(8,128)(2,1)S(1)}, u32[]{:S(2)}, u32[]{:S(2)}) collective-permute-start(bf16[2,4,2,4,64,128]{5,4,3,2,1,0:T(8,128)(2,1)S(1)} %bitcast.17), channel_id=1, source_target_pairs={{0,1},{1,0},{2,3},{3,2},{4,5},{5,4},{6,7},{7,6},{8,9},{9,8},{10,11... | collective-permute-start | bytes 3145736 | tf_op jit(solution)/shard_map/ppermute | solution.py:395
  104.7 12.5 %collective-permute-start.14 = (bf16[2,4,64,128]{3,2,1,0:T(8,128)(2,1)S(1)}, bf16[2,4,64,128]{3,2,1,0:T(8,128)(2,1)S(1)}, u32[]{:S(2)}, u32[]{:S(2)}) collective-permute-start(bf16[2,4,64,128]{3,2,1,0:T(8,128)(2,1)S(1)} %get-tuple-element.72), channel_id=1, source_target_pairs={{0,4},{4,8},{8,12},{12,0},{1,5},{5,9},{9,13},{13,1},{2,6},{6,10},{... | collective-permute-start | bytes 393224 | tf_op jit(solution)/shard_map/ppermute | solution.py:388
  107.7 10.6 %collective-permute-start.15 = (bf16[2,4,64,128]{3,2,1,0:T(8,128)(2,1)S(1)}, bf16[2,4,64,128]{3,2,1,0:T(8,128)(2,1)S(1)}, u32[]{:S(2)}, u32[]{:S(2)}) collective-permute-start(bf16[2,4,64,128]{3,2,1,0:T(8,128)(2,1)S(1)} %get-tuple-element.73), channel_id=1, source_target_pairs={{0,8},{4,12},{8,0},{12,4},{1,9},{5,13},{9,1},{13,5},{2,10},{6,14},... | collective-permute-start | bytes 393224 | tf_op jit(solution)/shard_map/ppermute | solution.py:388
  108.9 9.3 %collective-permute-start.16 = (bf16[2,4,64,128]{3,2,1,0:T(8,128)(2,1)S(1)}, bf16[2,4,64,128]{3,2,1,0:T(8,128)(2,1)S(1)}, u32[]{:S(2)}, u32[]{:S(2)}) collective-permute-start(bf16[2,4,64,128]{3,2,1,0:T(8,128)(2,1)S(1)} %get-tuple-element.74), channel_id=1, source_target_pairs={{0,12},{4,0},{8,4},{12,8},{1,13},{5,1},{9,5},{13,9},{2,14},{6,2},{... | collective-permute-start | bytes 393224 | tf_op jit(solution)/shard_map/ppermute | solution.py:388
  109.7 12.7 %collective-permute-start.21 = (bf16[4,2,4,64,128]{4,3,2,1,0:T(8,128)(2,1)S(1)}, bf16[4,2,4,64,128]{4,3,2,1,0:T(8,128)(2,1)S(1)}, u32[]{:S(2)}, u32[]{:S(2)}) collective-permute-start(bf16[4,2,4,64,128]{4,3,2,1,0:T(8,128)(2,1)S(1)} %join_pieces.11.rest_2_), channel_id=1, source_target_pairs={{0,2},{1,3},{2,0},{3,1},{4,6},{5,7},{6,4},{7,5},{8,10},{9,11},{10,... | collective-permute-start | bytes 1572872 | tf_op jit(solution)/shard_map/ppermute | solution.py:395
  118.8 14.9 %collective-permute-start.19 = (bf16[4,2,4,64,128]{4,3,2,1,0:T(8,128)(2,1)S(1)}, bf16[4,2,4,64,128]{4,3,2,1,0:T(8,128)(2,1)S(1)}, u32[]{:S(2)}, u32[]{:S(2)}) collective-permute-start(bf16[4,2,4,64,128]{4,3,2,1,0:T(8,128)(2,1)S(1)} %join_pieces.13.rest_2_), channel_id=1, source_target_pairs={{0,2},{1,3},{2,0},{3,1},{4,6},{5,7},{6,4},{7,5},{8,10},{9,11},{10,... | collective-permute-start | bytes 1572872 | tf_op jit(solution)/shard_map/ppermute | solution.py:395
  123.1 12.9 %collective-permute-start.22 = (bf16[2,4,2,4,64,128]{5,4,3,2,1,0:T(8,128)(2,1)S(1)}, bf16[2,4,2,4,64,128]{5,4,3,2,1,0:T(8,128)(2,1)S(1)}, u32[]{:S(2)}, u32[]{:S(2)}) collective-permute-start(bf16[2,4,2,4,64,128]{5,4,3,2,1,0:T(8,128)(2,1)S(1)} %bitcast.19), channel_id=1, source_target_pairs={{0,1},{1,0},{2,3},{3,2},{4,5},{5,4},{6,7},{7,6},{8,9},{9,8},{10,11... | collective-permute-start | bytes 3145736 | tf_op jit(solution)/shard_map/ppermute | solution.py:395
  134.3 8.8 %collective-permute-start.20 = (bf16[2,4,2,4,64,128]{5,4,3,2,1,0:T(8,128)(2,1)S(1)}, bf16[2,4,2,4,64,128]{5,4,3,2,1,0:T(8,128)(2,1)S(1)}, u32[]{:S(2)}, u32[]{:S(2)}) collective-permute-start(bf16[2,4,2,4,64,128]{5,4,3,2,1,0:T(8,128)(2,1)S(1)} %bitcast.21), channel_id=1, source_target_pairs={{0,1},{1,0},{2,3},{3,2},{4,5},{5,4},{6,7},{7,6},{8,9},{9,8},{10,11... | collective-permute-start | bytes 3145736 | tf_op jit(solution)/shard_map/ppermute | solution.py:395
